TPU v7x, 32 devices: a whole 2x2x4 slice. The times are simulated.
32 devices in a mesh: dp: 8 (over y, x, core), mp: 4 (over z).
Axes of the slice: x: 2, y: 2, z: 4, core: 2. Of those that a mesh axis runs over, the one named last changes fastest.
Arguments:
- inputs: bfloat16 [32768, 1024], P('dp'), may hold values from -6 to 6
- text_states: bfloat16 [32, 128, 1024], P('dp'), may hold values from -6 to 6
- text_lengths: int32 [32], P('dp'), may hold values from 8 to 128, as said below
- norm1_gain: float32 [1024], replicated, may hold values from 0.1 to 1.9
- norm1_bias: float32 [1024], replicated, may hold values from -2.5 to 2.5
- self_query: bfloat16 [1024, 1024], P(None, 'mp'), may hold values from -0.1875 to 0.1875
- self_key: bfloat16 [1024, 1024], P(None, 'mp'), may hold values from -0.1875 to 0.1875
- self_value: bfloat16 [1024, 1024], P(None, 'mp'), may hold values from -0.1875 to 0.1875
- self_out: bfloat16 [1024, 1024], P('mp'), may hold values from -3 to 3
- self_out_bias: float32 [1024], replicated, may hold values from -2.5 to 2.5
- norm2_gain: float32 [1024], replicated, may hold values from 0.1 to 1.9
- norm2_bias: float32 [1024], replicated, may hold values from -2.5 to 2.5
- cross_query: bfloat16 [1024, 1024], P(None, 'mp'), may hold values from -0.1875 to 0.1875
- cross_key: bfloat16 [1024, 1024], P(None, 'mp'), may hold values from -0.1875 to 0.1875
- cross_value: bfloat16 [1024, 1024], P(None, 'mp'), may hold values from -0.1875 to 0.1875
- cross_out: bfloat16 [1024, 1024], P('mp'), may hold values from -1 to 1
- cross_out_bias: float32 [1024], replicated, may hold values from -2.5 to 2.5
- norm3_gain: float32 [1024], replicated, may hold values from 0.1 to 1.9
- norm3_bias: float32 [1024], replicated, may hold values from -2.5 to 2.5
- mlp_in: bfloat16 [1024, 4096], P(None, 'mp'), may hold values from -0.1875 to 0.1875
- mlp_in_bias: float32 [4096], P('mp'), may hold values from -4 to 4
- mlp_out: bfloat16 [4096, 1024], P('mp'), may hold values from -0.125 to 0.125
- mlp_out_bias: float32 [1024], replicated, may hold values from -2.5 to 2.5
- cotangent: bfloat16 [32768, 1024], P('dp'), may hold values from -6 to 6
Outputs:
- output: bfloat16 [32768, 1024], P('dp')
- input_grad: bfloat16 [32768, 1024], P('dp')
- text_grad: float32 [32, 128, 1024], P('dp')
- norm1_gain_grad: float32 [1024], replicated
- norm1_bias_grad: float32 [1024], replicated
- self_query_grad: float32 [1024, 1024], P(None, 'mp')
- self_key_grad: float32 [1024, 1024], P(None, 'mp')
- self_value_grad: float32 [1024, 1024], P(None, 'mp')
- self_out_grad: float32 [1024, 1024], P('mp')
- self_out_bias_grad: float32 [1024], replicated
- norm2_gain_grad: float32 [1024], replicated
- norm2_bias_grad: float32 [1024], replicated
- cross_query_grad: float32 [1024, 1024], P(None, 'mp')
- cross_key_grad: float32 [1024, 1024], P(None, 'mp')
- cross_value_grad: float32 [1024, 1024], P(None, 'mp')
- cross_out_grad: float32 [1024, 1024], P('mp')
- cross_out_bias_grad: float32 [1024], replicated
- norm3_gain_grad: float32 [1024], replicated
- norm3_bias_grad: float32 [1024], replicated
- mlp_in_grad: float32 [1024, 4096], P(None, 'mp')
- mlp_in_bias_grad: float32 [4096], P('mp')
- mlp_out_grad: float32 [4096, 1024], P('mp')
- mlp_out_bias_grad: float32 [1024], replicated
Inputs may be any that keep to these rules, and one draw needn't show every extreme that they name: `text_lengths`: valid text slots of each item; the slots after them are padding. Some item has all 128.
All inputs are finite; a program needn't handle non-finite values.
Results may differ from a plain program's by a relative error of at most 0.02.
The roundings to bfloat16 on the way count: a program that leaves them out, or rounds other values in their place, can miss the bound.
Values may be sent and summed in bfloat16 or wider, within the bound.
No kernel may reach another device: no remote copies, remote signals or barrier semaphores. Data moves between devices by JAX's collectives and lax.ppermute only.
A program may use at most 448 MiB of HBM per device.

v0:
```python
import jax
import jax.numpy as jnp
from jax import lax
from jax.sharding import PartitionSpec as P

HEAD_DIM = 64
TXT = 128
SEQ = 1024


epsilon = 1e-05


def layer_stats(hidden):
    average = jnp.mean(hidden, axis=-1, keepdims=True)
    center = hidden - average
    variance = jnp.mean(center * center, axis=-1, keepdims=True)
    inverse = lax.rsqrt(variance + epsilon)
    return (center * inverse, inverse)


def norm_back(upstream, scaled, inverse, gain_vector):
    tilted = upstream * gain_vector
    return inverse * (
        tilted
        - jnp.mean(tilted, axis=-1, keepdims=True)
        - scaled * jnp.mean(tilted * scaled, axis=-1, keepdims=True)
    )


def left_product(left_side, right_side):
    return lax.dot_general(
        left_side, right_side, (((0,), (0,)), ((), ())), preferred_element_type=jnp.float32
    )


def right_product(left_side, right_side):
    return lax.dot_general(
        left_side, right_side, (((1,), (1,)), ((), ())), preferred_element_type=jnp.float32
    )


def forward_rows(values, weight, share_rows):
    piece_rows = lax.dynamic_slice_in_dim(values, jnp.int32(0), share_rows * lax.axis_size("mp"), 0)
    return lax.psum_scatter(
        jnp.dot(piece_rows, weight, preferred_element_type=jnp.float32),
        "mp",
        scatter_dimension=0,
        tiled=True,
    )


def backward_rows(factor_pairs, share_rows):
    offset = jnp.int32(0)
    count_rows = share_rows * lax.axis_size("mp")
    running = None
    for left_side, right_side in factor_pairs:
        piece_rows = lax.dynamic_slice_in_dim(left_side, offset, count_rows, 0)
        addend = right_product(piece_rows, right_side)
        running = addend if running is None else running + addend
    return lax.psum_scatter(running, "mp", scatter_dimension=0, tiled=True)


def block_mask(offset, block_rows, key_count, item_length, causal):
    query_pos = offset + jnp.arange(block_rows)[:, None]
    key_pos = jnp.arange(key_count)[None, :]
    if causal:
        return query_pos >= key_pos
    return jnp.broadcast_to(key_pos < item_length, (block_rows, key_count))


def attend_forward(queries, key_rows, value_rows, lengths, causal):
    seq_rows = queries.shape[1]
    key_count = key_rows.shape[1]
    block_rows = min(512, seq_rows)
    scaling = HEAD_DIM ** (-0.5)

    def one_item(packed):
        item_query, item_keys, item_values, item_length = packed
        results = []
        totals = []
        for offset in range(0, seq_rows, block_rows):
            allowed = block_mask(offset, block_rows, key_count, item_length, causal)
            scores = (
                jnp.einsum(
                    "qhe,khe->hqk",
                    item_query[offset : offset + block_rows],
                    item_keys,
                    preferred_element_type=jnp.float32,
                )
                * scaling
            )
            scores = jnp.where(allowed[None], scores, -1e30)
            highest = jnp.max(scores, axis=-1, keepdims=True)
            weights = jnp.exp(scores - highest)
            row_total = jnp.sum(weights, axis=-1, keepdims=True)
            shares = (weights / row_total).astype(jnp.bfloat16)
            results.append(
                jnp.einsum("hqk,khe->qhe", shares, item_values, preferred_element_type=jnp.float32)
            )
            totals.append(highest + jnp.log(row_total))
        return (jnp.concatenate(results, 0).astype(jnp.bfloat16), jnp.concatenate(totals, 1))

    return lax.map(one_item, (queries, key_rows, value_rows, lengths))


def attend_backward(queries, key_rows, value_rows, lengths, sums_kept, grad_out, causal):
    seq_rows = queries.shape[1]
    key_count = key_rows.shape[1]
    block_rows = min(512, seq_rows)
    scaling = HEAD_DIM ** (-0.5)

    def one_item(packed):
        item_query, item_keys, item_values, item_length, item_sums, item_grad = packed
        query_grads = []
        key_grad = jnp.zeros(item_keys.shape, jnp.float32)
        value_grad = jnp.zeros(item_values.shape, jnp.float32)
        for offset in range(0, seq_rows, block_rows):
            block_query = item_query[offset : offset + block_rows]
            block_grad = item_grad[offset : offset + block_rows]
            allowed = block_mask(offset, block_rows, key_count, item_length, causal)
            scores = (
                jnp.einsum(
                    "qhe,khe->hqk", block_query, item_keys, preferred_element_type=jnp.float32
                )
                * scaling
            )
            scores = jnp.where(allowed[None], scores, -1e30)
            shares = jnp.exp(scores - item_sums[:, offset : offset + block_rows])
            rounded = shares.astype(jnp.bfloat16)
            value_grad = value_grad + jnp.einsum(
                "hqk,qhe->khe", rounded, block_grad, preferred_element_type=jnp.float32
            )
            share_grad = jnp.einsum(
                "qhe,khe->hqk", block_grad, item_values, preferred_element_type=jnp.float32
            )
            score_grad = (
                shares * (share_grad - jnp.sum(shares * share_grad, axis=-1, keepdims=True))
            ).astype(jnp.bfloat16)
            query_part = (
                jnp.einsum(
                    "hqk,khe->qhe", score_grad, item_keys, preferred_element_type=jnp.float32
                )
                * scaling
            )
            query_grads.append(query_part.astype(jnp.bfloat16))
            key_grad = (
                key_grad
                + jnp.einsum(
                    "hqk,qhe->khe", score_grad, block_query, preferred_element_type=jnp.float32
                )
                * scaling
            )
        return (
            jnp.concatenate(query_grads, 0),
            key_grad.astype(jnp.bfloat16),
            value_grad.astype(jnp.bfloat16),
        )

    return lax.map(one_item, (queries, key_rows, value_rows, lengths, sums_kept, grad_out))


def gelu_exact(values):
    return jax.nn.gelu(values, approximate=False)


def on_device(
    inputs,
    text_states,
    text_lengths,
    norm1_gain,
    norm1_bias,
    self_query,
    self_key,
    self_value,
    self_out,
    self_out_bias,
    norm2_gain,
    norm2_bias,
    cross_query,
    cross_key,
    cross_value,
    cross_out,
    cross_out_bias,
    norm3_gain,
    norm3_bias,
    mlp_in,
    mlp_in_bias,
    mlp_out,
    mlp_out_bias,
    cotangent,
):
    bf16 = jnp.bfloat16
    row_count = inputs.shape[0]
    item_count = text_states.shape[0]
    share_rows = row_count // lax.axis_size("mp")
    first_row = lax.axis_index("mp") * share_rows
    tokens = inputs.astype(jnp.float32)
    texts_flat = text_states.reshape(item_count * TXT, text_states.shape[2])
    grad_top = cotangent.astype(jnp.float32)

    def rows_of(whole):
        return lax.dynamic_slice_in_dim(whole, first_row, share_rows, 0)

    def split_heads(flat_rows, length):
        return flat_rows.reshape(item_count, length, flat_rows.shape[1] // HEAD_DIM, HEAD_DIM)

    def add_branch(residual, branch_rows, bias_add):
        return residual + lax.all_gather(branch_rows, "mp", axis=0, tiled=True) + bias_add

    def norm_backward(part_rows, residual_grad, scaled, inverse, gain_vector):
        upstream = lax.all_gather(part_rows, "mp", axis=0, tiled=True)
        whole_grad = residual_grad + norm_back(upstream, scaled, inverse, gain_vector)
        scaled_rows = rows_of(scaled)
        return (whole_grad, jnp.sum(part_rows * scaled_rows, 0), jnp.sum(part_rows, 0))

    scaled_one, inverse_one = layer_stats(tokens)
    normed_self = (scaled_one * norm1_gain + norm1_bias).astype(bf16)
    self_queries = split_heads(
        jnp.dot(normed_self, self_query, preferred_element_type=jnp.float32).astype(bf16), SEQ
    )
    self_keys = split_heads(
        jnp.dot(normed_self, self_key, preferred_element_type=jnp.float32).astype(bf16), SEQ
    )
    self_values = split_heads(
        jnp.dot(normed_self, self_value, preferred_element_type=jnp.float32).astype(bf16), SEQ
    )
    self_mixed, self_sums = attend_forward(self_queries, self_keys, self_values, text_lengths, True)
    self_mixed = self_mixed.reshape(row_count, -1)
    hidden_one = add_branch(tokens, forward_rows(self_mixed, self_out, share_rows), self_out_bias)
    scaled_two, inverse_two = layer_stats(hidden_one)
    normed_cross = (scaled_two * norm2_gain + norm2_bias).astype(bf16)
    cross_queries = split_heads(
        jnp.dot(normed_cross, cross_query, preferred_element_type=jnp.float32).astype(bf16), SEQ
    )
    cross_keys = split_heads(
        jnp.dot(texts_flat, cross_key, preferred_element_type=jnp.float32).astype(bf16), TXT
    )
    cross_values = split_heads(
        jnp.dot(texts_flat, cross_value, preferred_element_type=jnp.float32).astype(bf16), TXT
    )
    cross_mixed, cross_sums = attend_forward(
        cross_queries, cross_keys, cross_values, text_lengths, False
    )
    cross_mixed = cross_mixed.reshape(row_count, -1)
    hidden_two = add_branch(
        hidden_one, forward_rows(cross_mixed, cross_out, share_rows), cross_out_bias
    )
    scaled_three, inverse_three = layer_stats(hidden_two)
    normed_mlp = (scaled_three * norm3_gain + norm3_bias).astype(bf16)
    inner = jnp.dot(normed_mlp, mlp_in, preferred_element_type=jnp.float32) + mlp_in_bias
    active = gelu_exact(inner).astype(bf16)
    hidden_three = add_branch(hidden_two, forward_rows(active, mlp_out, share_rows), mlp_out_bias)
    output = hidden_three.astype(bf16)
    mlp_out_grad = left_product(active, cotangent)
    mlp_out_bias_grad = jnp.sum(rows_of(grad_top), 0)
    active_grad = right_product(cotangent, mlp_out)
    inner_value, gelu_back = jax.vjp(gelu_exact, inner)
    inner_grad = gelu_back(active_grad)[0].astype(bf16)
    mlp_in_bias_grad = jnp.sum(inner_grad.astype(jnp.float32), 0)
    mlp_in_grad = left_product(normed_mlp, inner_grad)
    part_rows = backward_rows(((inner_grad, mlp_in),), share_rows)
    hidden_two_grad, norm3_gain_grad, norm3_bias_grad = norm_backward(
        part_rows, grad_top, scaled_three, inverse_three, norm3_gain
    )
    branch_grad = hidden_two_grad.astype(bf16)
    cross_out_grad = left_product(cross_mixed, branch_grad)
    cross_out_bias_grad = jnp.sum(rows_of(branch_grad).astype(jnp.float32), 0)
    mixed_grad = right_product(branch_grad, cross_out).astype(bf16)
    query_grad, key_grad, value_grad = attend_backward(
        cross_queries,
        cross_keys,
        cross_values,
        text_lengths,
        cross_sums,
        split_heads(mixed_grad, SEQ),
        False,
    )
    query_grad = query_grad.reshape(row_count, -1)
    key_grad = key_grad.reshape(item_count * TXT, -1)
    value_grad = value_grad.reshape(item_count * TXT, -1)
    cross_query_grad = left_product(normed_cross, query_grad)
    cross_key_grad = left_product(texts_flat, key_grad)
    cross_value_grad = left_product(texts_flat, value_grad)
    text_part = right_product(key_grad, cross_key) + right_product(value_grad, cross_value)
    text_grad = lax.psum(text_part, "mp").reshape(text_states.shape)
    part_rows = backward_rows(((query_grad, cross_query),), share_rows)
    hidden_one_grad, norm2_gain_grad, norm2_bias_grad = norm_backward(
        part_rows, hidden_two_grad, scaled_two, inverse_two, norm2_gain
    )
    branch_grad = hidden_one_grad.astype(bf16)
    self_out_grad = left_product(self_mixed, branch_grad)
    self_out_bias_grad = jnp.sum(rows_of(branch_grad).astype(jnp.float32), 0)
    mixed_grad = right_product(branch_grad, self_out).astype(bf16)
    query_grad, key_grad, value_grad = attend_backward(
        self_queries,
        self_keys,
        self_values,
        text_lengths,
        self_sums,
        split_heads(mixed_grad, SEQ),
        True,
    )
    query_grad = query_grad.reshape(row_count, -1)
    key_grad = key_grad.reshape(row_count, -1)
    value_grad = value_grad.reshape(row_count, -1)
    self_query_grad = left_product(normed_self, query_grad)
    self_key_grad = left_product(normed_self, key_grad)
    self_value_grad = left_product(normed_self, value_grad)
    part_rows = backward_rows(
        ((query_grad, self_query), (key_grad, self_key), (value_grad, self_value)), share_rows
    )
    input_whole, norm1_gain_grad, norm1_bias_grad = norm_backward(
        part_rows, hidden_one_grad, scaled_one, inverse_one, norm1_gain
    )
    input_grad = input_whole.astype(bf16)
    (
        self_query_grad,
        self_key_grad,
        self_value_grad,
        self_out_grad,
        cross_query_grad,
        cross_key_grad,
        cross_value_grad,
        cross_out_grad,
        mlp_in_grad,
        mlp_in_bias_grad,
        mlp_out_grad,
    ) = lax.psum(
        (
            self_query_grad,
            self_key_grad,
            self_value_grad,
            self_out_grad,
            cross_query_grad,
            cross_key_grad,
            cross_value_grad,
            cross_out_grad,
            mlp_in_grad,
            mlp_in_bias_grad,
            mlp_out_grad,
        ),
        "dp",
    )
    (
        norm1_gain_grad,
        norm1_bias_grad,
        self_out_bias_grad,
        norm2_gain_grad,
        norm2_bias_grad,
        cross_out_bias_grad,
        norm3_gain_grad,
        norm3_bias_grad,
        mlp_out_bias_grad,
    ) = lax.psum(
        (
            norm1_gain_grad,
            norm1_bias_grad,
            self_out_bias_grad,
            norm2_gain_grad,
            norm2_bias_grad,
            cross_out_bias_grad,
            norm3_gain_grad,
            norm3_bias_grad,
            mlp_out_bias_grad,
        ),
        ("dp", "mp"),
    )
    return (
        output,
        input_grad,
        text_grad,
        norm1_gain_grad,
        norm1_bias_grad,
        self_query_grad,
        self_key_grad,
        self_value_grad,
        self_out_grad,
        self_out_bias_grad,
        norm2_gain_grad,
        norm2_bias_grad,
        cross_query_grad,
        cross_key_grad,
        cross_value_grad,
        cross_out_grad,
        cross_out_bias_grad,
        norm3_gain_grad,
        norm3_bias_grad,
        mlp_in_grad,
        mlp_in_bias_grad,
        mlp_out_grad,
        mlp_out_bias_grad,
    )


def solution(mesh):
    return jax.shard_map(
        on_device,
        mesh=mesh,
        in_specs=(
            P("dp", None),
            P("dp", None, None),
            P("dp"),
            P(),
            P(),
            P(None, "mp"),
            P(None, "mp"),
            P(None, "mp"),
            P("mp", None),
            P(),
            P(),
            P(),
            P(None, "mp"),
            P(None, "mp"),
            P(None, "mp"),
            P("mp", None),
            P(),
            P(),
            P(),
            P(None, "mp"),
            P("mp"),
            P("mp", None),
            P(),
            P("dp", None),
        ),
        out_specs=(
            P("dp", None),
            P("dp", None),
            P("dp", None, None),
            P(),
            P(),
            P(None, "mp"),
            P(None, "mp"),
            P(None, "mp"),
            P("mp", None),
            P(),
            P(),
            P(),
            P(None, "mp"),
            P(None, "mp"),
            P(None, "mp"),
            P("mp", None),
            P(),
            P(),
            P(),
            P(None, "mp"),
            P("mp"),
            P("mp", None),
            P(),
        ),
        check_vma=False,
    )
```

profile of v0, /device:TPU:0, one launch (start us, length us, event | category | flops | bytes accessed | tf_op | source)
XLA Modules:
  0.0 4272.9 jit_solution(13296398870183764356)
XLA Ops:
  30.0 7.1 reshape.438
  37.1 7.0 copy.84
  44.1 7.0 convolution_convert_fusion.6
  51.2 7.1 reshape.437
  58.3 7.0 copy.83
  65.3 7.0 convolution_convert_fusion.7
  72.4 7.2 reshape.436
  88.1 68.7 %while.52 = (s32[]{:T(128)}, bf16[4,1024,4,64]{1,3,2,0:T(8,128)(2,1)}, f32[4,4,1024,1]{2,1,3,0:T(4,128)S(1)}, bf16[4,1024,4,64]{1,3,2,0:T(8,128)(2,1)}, bf16[4,1...) while((s32[]{:T(128)}, ...), condition=%wide.region_7.8_spmd, body=%wide.region_2.7_spmd.sunk | while | flops 1126433280 | bytes 67279520 | solution.py:104
  162.3 8.2 fusion.186
  170.6 283.1 %reduce-scatter.7.cloned.1.call-done = f32[1024,1024]{1,0:T(8,128)} async-done(((f32[4096,1024]{1,0:T(8,128)}), f32[1024,1024]{1,0:T(8,128)}) %reduce-scatter.7.cloned.1.call-update) | async-done | bytes 4194320 | tf_op jit(solution)/shard_map/reduce_scatter | solution.py:45
  461.3 281.6 %all-gather.7.cloned.1.call-done = f32[4096,1024]{1,0:T(8,128)} async-done(((f32[1024,1024]{1,0:T(8,128)}), f32[4096,1024]{1,0:T(8,128)}) %all-gather.7.cloned.1.call-update) | async-done | bytes 16777232 | tf_op jit(solution)/shard_map/all_gather | solution.py:209
  742.9 9.7 fusion.176
  769.3 9.6 convolution_convert_fusion.4
  778.9 7.1 reshape.440
  786.0 7.0 copy.90
  794.6 35.2 while.53
  835.5 8.1 fusion.187
  843.7 278.6 %reduce-scatter.9.cloned.1.call-done = f32[1024,1024]{1,0:T(8,128)} async-done(((f32[4096,1024]{1,0:T(8,128)}), f32[1024,1024]{1,0:T(8,128)}) %reduce-scatter.9.cloned.1.call-update) | async-done | bytes 4194320 | tf_op jit(solution)/shard_map/reduce_scatter | solution.py:45
  1122.3 288.9 %all-gather.9.cloned.1.call-done = f32[4096,1024]{1,0:T(8,128)} async-done(((f32[1024,1024]{1,0:T(8,128)}), f32[4096,1024]{1,0:T(8,128)}) %all-gather.9.cloned.1.call-update) | async-done | bytes 16777232 | tf_op jit(solution)/shard_map/all_gather | solution.py:209
  1411.2 14.3 fusion.183
  1439.0 18.6 fusion.166
  1457.6 50.8 %convert_reduce_fusion.1 = (f32[1024]{0:T(1024)}, bf16[4096,1024]{1,0:T(8,128)(2,1)S(1)}, f32[4096,1024]{1,0:T(8,128)}) fusion(f32[4096,1024]{1,0:T(8,128)} %fusion.166, f32[1024]{0:T(1024)S(1)} %copy-done.78, bf16[4096,1024]{1,0:T(8,128)(2,1)S(1)} %bitcast.473, bf16[1024,1024]{1,0:T(8,128)(2,1)S(1)} %copy-done), kind=kOutput, calls=%fused_computation.222 | convolution fusion | flops 8904506368 | bytes 52436992 | tf_op jit(solution)/shard_map/dot_general | solution.py:38
  1511.7 11.7 fusion.189
  1523.5 278.6 %reduce-scatter.13.cloned.1.call-done = f32[1024,1024]{1,0:T(8,128)} async-done(((f32[4096,1024]{1,0:T(8,128)}), f32[1024,1024]{1,0:T(8,128)}) %reduce-scatter.13.cloned.1.call-update) | async-done | bytes 4194320 | tf_op jit(solution)/shard_map/reduce_scatter | solution.py:61
  1802.2 289.0 %all-gather.13.cloned.1.call-done = f32[4096,1024]{1,0:T(8,128)} async-done(((f32[1024,1024]{1,0:T(8,128)}), f32[4096,1024]{1,0:T(8,128)}) %all-gather.13.cloned.1.call-update) | async-done | bytes 16777232 | tf_op jit(solution)/shard_map/all_gather | solution.py:212
  2091.2 12.6 multiply_reduce_fusion.11
  2106.5 17.8 fusion.182
  2124.3 7.1 convolution_convert_fusion.3
  2131.4 7.1 reshape.434
  2138.5 7.0 copy.96
  2147.1 62.6 %while.54 = (s32[]{:T(128)}, bf16[4,1024,4,64]{1,3,2,0:T(8,128)(2,1)}, bf16[4,128,4,64]{1,3,2,0:T(8,128)(2,1)}, bf16[4,128,4,64]{1,3,2,0:T(8,128)(2,1)}, bf16[4,...) while((s32[]{:T(128)}, ...), condition=%wide.region_27.28_spmd, body=%wide.region_24.27_spmd.sunk | while | flops 341995648 | bytes 20571448 | solution.py:160
  2215.3 8.1 fusion.190
  2223.5 278.6 %reduce-scatter.15.cloned.1.call-done = f32[1024,1024]{1,0:T(8,128)} async-done(((f32[4096,1024]{1,0:T(8,128)}), f32[1024,1024]{1,0:T(8,128)}) %reduce-scatter.15.cloned.1.call-update) | async-done | bytes 4194320 | tf_op jit(solution)/shard_map/reduce_scatter | solution.py:61
  2502.2 12.7 multiply_convert_fusion.4
  2518.8 11.7 fusion.188
  2530.6 260.6 %all-gather.15.cloned.1.call-done = f32[4096,1024]{1,0:T(8,128)} async-done(((f32[1024,1024]{1,0:T(8,128)}), f32[4096,1024]{1,0:T(8,128)}) %all-gather.15.cloned.1.call-update) | async-done | bytes 16777232 | tf_op jit(solution)/shard_map/all_gather | solution.py:212
  2791.2 12.9 multiply_reduce_fusion.10
  2804.1 23.6 fusion.181
  2836.7 7.0 copy.102
  2848.5 165.9 %while.55 = (s32[]{:T(128)}, bf16[4,1024,4,64]{1,3,2,0:T(8,128)(2,1)}, bf16[4,1024,4,64]{1,3,2,0:T(8,128)(2,1)}, bf16[4,1024,4,64]{1,3,2,0:T(8,128)(2,1)}, bf16[...) while((s32[]{:T(128)}, ...), condition=%wide.region_34.35_spmd, body=%wide.region_31.34_spmd.sunk | while | flops 2751197696 | bytes 159018704 | solution.py:160
  2871.6 8.4 multiply_convert_fusion.10
  2912.9 8.4 multiply_convert_fusion.10
  2954.3 8.3 multiply_convert_fusion.10
  2995.6 8.4 multiply_convert_fusion.10
  3025.1 8.1 fusion.192
  3033.3 8.4 fusion.191
  3041.7 19.0 add_add_fusion
  3060.8 11.3 reduce-scatter.11.cloned.1.call-done
  3072.2 15.0 fusion.198
  3087.3 16.8 fusion.165
  3107.4 7.0 fusion.197
  3124.8 7.0 fusion.195
  3131.8 7.1 fusion.193
  3142.4 213.1 %reduce-scatter.17.cloned.1.call-done = f32[1024,1024]{1,0:T(8,128)} async-done(((f32[4096,1024]{1,0:T(8,128)}), f32[1024,1024]{1,0:T(8,128)}) %reduce-scatter.17.cloned.1.call-update) | async-done | bytes 4194320 | tf_op jit(solution)/shard_map/reduce_scatter | solution.py:61
  3355.6 13.0 convert_element_type.178
  3371.7 14.5 psum.165
  3395.7 248.8 %all-gather.11.cloned.1.call-done = f32[4096,1024]{1,0:T(8,128)} async-done(((f32[1024,1024]{1,0:T(8,128)}), f32[4096,1024]{1,0:T(8,128)}) %all-gather.11.cloned.1.call-update) | async-done | bytes 16777232 | tf_op jit(solution)/shard_map/all_gather | solution.py:209
  3644.6 15.8 add_convert_fusion.2
  3665.4 207.8 %all-reduce.7.cloned.1.call-done = (f32[1024,256]{1,0:T(8,128)}, f32[1024,256]{1,0:T(8,128)}, f32[1024,256]{1,0:T(8,128)}, f32[256,1024]{1,0:T(8,128)}, f32[1024...) async-done(((f32[1024,256]{1,0:T(8,128)}, f32[1024,256]{1,0:T(8,128)}, ...) | async-done | bytes 16777232 | tf_op jit(solution)/shard_map/psum | solution.py:329
  3882.6 55.4 %all-reduce = (f32[1024]{0:T(1024)}, f32[1024]{0:T(1024)}, f32[1024]{0:T(1024)}, f32[1024]{0:T(1024)}, f32[1024]{0:T(1024)}, /*index=5*/f32[1024]{0:T(1024)}, f32[1024]{0:T(1024)}, f32[1024]{0:T(1024)}, f32[1024]{0:T(1024)}) all-reduce(f32[1024]{0:T(1024)S(1)} %get-tuple-element.328, ...), channel_id=1, replica_groups=mesh['dp'=8,'mp'=4] {'dp','mp'}, use_global_device_ids=true, to_apply=%region_40.41 | all-reduce | flops 9216 | bytes 73728 | tf_op jit(solution)/shard_map/psum | solution.py:355
  3938.0 224.7 %all-gather.17.cloned.1.call-done = f32[4096,1024]{1,0:T(8,128)} async-done(((f32[1024,1024]{1,0:T(8,128)}), f32[4096,1024]{1,0:T(8,128)}) %all-gather.17.cloned.1.call-update) | async-done | bytes 16777232 | tf_op jit(solution)/shard_map/all_gather | solution.py:212
  4162.7 11.2 multiply_reduce_fusion.9
  4176.2 13.3 add_convert_fusion
  4189.5 60.9 %all-reduce.5.cloned.1.call-done = f32[4,128,1024]{2,1,0:T(8,128)} async-done(((f32[4,128,1024]{2,1,0:T(8,128)}), f32[4,128,1024]{2,1,0:T(8,128)}) %all-reduce.5.cloned.1.call-update) | async-done | bytes 2097168 | tf_op jit(solution)/shard_map/psum | solution.py:286
  (546 shorter events, 471.1 us)
Async XLA Ops:
  7.2 1450.4 %copy-start = (bf16[1024,1024]{1,0:T(8,128)(2,1)S(1)}, bf16[1024,1024]{1,0:T(8,128)(2,1)}, u32[]{:S(2)}) copy-start(bf16[1024,1024]{1,0:T(8,128)(2,1)} %param.53) | copy-start | bytes 6291460
  7.2 446.5 %reduce-scatter.7.cloned.1.call-start = ((), (), s32[]{:S(2)}) async-start(), calls=%async_computation.6 | async-start | bytes 20971520 | tf_op jit(solution)/shard_map/reduce_scatter | solution.py:45
  30.0 14.1 copy-start.49
  51.2 14.1 copy-start.39
  156.8 13.7 copy-start.57
  170.5 283.3 %copy-start.31 = (bf16[4,128,1024]{2,1,0:T(8,128)(2,1)S(1)}, bf16[4,128,1024]{2,1,0:T(8,128)(2,1)}, u32[]{:S(2)}) copy-start(bf16[4,128,1024]{2,1,0:T(8,128)(2,1)} %param.33) | copy-start | bytes 3145732
  170.5 572.3 %copy-start.66 = (f32[1024]{0:T(1024)S(1)}, f32[1024]{0:T(1024)}, u32[]{:S(2)}) copy-start(f32[1024]{0:T(1024)} %param.41) | copy-start | bytes 12292
  170.5 572.3 %all-gather.7.cloned.1.call-start = ((), (), s32[]{:S(2)}) async-start(), calls=%async_computation.7 | async-start | bytes 20971520 | tf_op jit(solution)/shard_map/all_gather | solution.py:209
  453.7 668.5 %reduce-scatter.9.cloned.1.call-start = ((), (), s32[]{:S(2)}) async-start(), calls=%async_computation.8 | async-start | bytes 20971520 | tf_op jit(solution)/shard_map/reduce_scatter | solution.py:45
  742.9 13.1 copy-start.4
  742.9 19.6 slice-start
  778.9 15.7 copy-start.85
  829.8 13.8 copy-start.9
  829.8 13.8 copy-start.33
  829.8 13.8 copy-start.56
  843.6 567.6 %copy-start.75 = (f32[1024]{0:T(1024)S(1)}, f32[1024]{0:T(1024)}, u32[]{:S(2)}) copy-start(f32[1024]{0:T(1024)} %param.48) | copy-start | bytes 12292
  843.6 567.6 %all-gather.9.cloned.1.call-start = ((), (), s32[]{:S(2)}) async-start(), calls=%async_computation.9 | async-start | bytes 20971520 | tf_op jit(solution)/shard_map/all_gather | solution.py:209
  1122.3 679.8 %reduce-scatter.13.cloned.1.call-start = ((), (), s32[]{:S(2)}) async-start(), calls=%async_computation.12 | async-start | bytes 20971520 | tf_op jit(solution)/shard_map/reduce_scatter | solution.py:61
  1432.3 25.3 slice-start.6
  1438.9 18.7 slice-start.7
  1439.0 18.7 copy-start.78
  1457.6 54.0 %copy-start.80 = (bf16[1024,1024]{1,0:T(8,128)(2,1)S(1)}, bf16[1024,1024]{1,0:T(8,128)(2,1)}, u32[]{:S(2)}) copy-start(bf16[1024,1024]{1,0:T(8,128)(2,1)} %param.51) | copy-start | bytes 6291460
  1523.4 567.8 %copy-start.55 = (f32[4096]{0:T(1024)S(1)}, f32[4096]{0:T(1024)}, u32[]{:S(2)}) copy-start(f32[4096]{0:T(1024)} %copy-done.54) | copy-start | bytes 49156
  1523.4 567.8 %copy-start.59 = (f32[4096]{0:T(1024)S(1)}, f32[4096]{0:T(1024)}, u32[]{:S(2)}) copy-start(f32[4096]{0:T(1024)} %copy-done.58) | copy-start | bytes 49156
  1523.4 567.8 %copy-start.70 = (f32[1024]{0:T(1024)S(1)}, f32[1024]{0:T(1024)}, u32[]{:S(2)}) copy-start(f32[1024]{0:T(1024)} %param.49) | copy-start | bytes 12292
  1523.4 567.7 %all-gather.13.cloned.1.call-start = ((), (), s32[]{:S(2)}) async-start(), calls=%async_computation.13 | async-start | bytes 20971520 | tf_op jit(solution)/shard_map/all_gather | solution.py:212
  1802.1 700.0 %reduce-scatter.15.cloned.1.call-start = ((), (), s32[]{:S(2)}) async-start(), calls=%async_computation.14 | async-start | bytes 20971520 | tf_op jit(solution)/shard_map/reduce_scatter | solution.py:61
  2091.2 15.4 copy-start.5
  2106.5 17.8 copy-start.42
  2131.4 15.7 copy-start.10
  2131.4 15.7 copy-start.34
  2131.4 15.7 copy-start.86
  2223.4 567.7 %all-gather.15.cloned.1.call-start = ((), (), s32[]{:S(2)}) async-start(), calls=%async_computation.15 | async-start | bytes 20971520 | tf_op jit(solution)/shard_map/all_gather | solution.py:212
  2502.1 570.0 %reduce-scatter.11.cloned.1.call-start = ((), (), s32[]{:S(2)}) async-start(), calls=%async_computation.10 | async-start | bytes 20971520 | tf_op jit(solution)/shard_map/reduce_scatter | solution.py:45
  2530.5 260.7 %copy-start.73 = (f32[1024]{0:T(1024)S(1)}, f32[1024]{0:T(1024)}, u32[]{:S(2)}) copy-start(f32[1024]{0:T(1024)} %param.42) | copy-start | bytes 12292
  2530.5 273.6 %copy-start.65 = (f32[4096]{0:T(1024)S(1)}, f32[4096]{0:T(1024)}, u32[]{:S(2)}) copy-start(f32[4096]{0:T(1024)} %copy-done.64) | copy-start | bytes 49156
  2530.6 824.9 %reduce-scatter.17.cloned.1.call-start = ((), (), s32[]{:S(2)}) async-start(), calls=%async_computation.16 | async-start | bytes 20971520 | tf_op jit(solution)/shard_map/reduce_scatter | solution.py:61
  2804.1 26.9 copy-start.46
  3060.7 583.9 %all-gather.11.cloned.1.call-start = ((), (), s32[]{:S(2)}) async-start(), calls=%async_computation.11 | async-start | bytes 20971520 | tf_op jit(solution)/shard_map/all_gather | solution.py:209
  3072.1 15.1 copy-start.71
  3072.1 15.1 copy-start.82
  3072.1 801.1 %all-reduce.7.cloned.1.call-start = ((), (), s32[]{:S(2)}) async-start(), calls=%async_computation.19 | async-start | bytes 33554432 | tf_op jit(solution)/shard_map/psum | solution.py:329
  3087.2 16.9 copy-start.62
  3087.2 17.1 copy-start.63
  3087.2 17.3 copy-start.32
  3087.3 20.1 copy-start.23
  3087.3 27.1 slice-start.2
  3087.3 27.1 slice-start.3
  3087.3 27.1 slice-start.4
  3124.8 14.1 slice-start.8
  3142.3 1020.4 %all-gather.17.cloned.1.call-start = ((), (), s32[]{:S(2)}) async-start(), calls=%async_computation.17 | async-start | bytes 20971520 | tf_op jit(solution)/shard_map/all_gather | solution.py:212
  3355.5 894.9 %all-reduce.5.cloned.1.call-start = ((), (), s32[]{:S(2)}) async-start(), calls=%async_computation.18 | async-start | bytes 4194304 | tf_op jit(solution)/shard_map/psum | solution.py:286
  3355.6 16.1 copy-start.76
  3368.6 25.3 copy-start.51
  3386.2 258.4 %copy-start.79 = (f32[1024]{0:T(1024)S(1)}, f32[1024]{0:T(1024)}, u32[]{:S(2)}) copy-start(f32[1024]{0:T(1024)} %param.54) | copy-start | bytes 12292
  3644.6 15.8 copy-start.11
  3663.4 499.3 %copy-start.53 = (f32[4096]{0:T(1024)S(1)}, f32[4096]{0:T(1024)}, u32[]{:S(2)}) copy-start(f32[4096]{0:T(1024)} %copy-done.52) | copy-start | bytes 49156
  3663.4 499.3 %copy-start.61 = (f32[4096]{0:T(1024)S(1)}, f32[4096]{0:T(1024)}, u32[]{:S(2)}) copy-start(f32[4096]{0:T(1024)} %copy-done.60) | copy-start | bytes 49156
  3663.4 499.3 %copy-start.68 = (f32[1024]{0:T(1024)S(1)}, f32[1024]{0:T(1024)}, u32[]{:S(2)}) copy-start(f32[1024]{0:T(1024)} %param.35) | copy-start | bytes 12292
  4162.7 13.4 copy-start.6
  4189.5 69.7 %copy-start.37 = (f32[256,1024]{1,0:T(8,128)S(1)}, f32[256,1024]{1,0:T(8,128)}, u32[]{:S(2)}) copy-start(f32[256,1024]{1,0:T(8,128)} %get-tuple-element.839) | copy-start | bytes 3145732
  4189.5 70.7 %copy-start.36 = (f32[1024,256]{1,0:T(8,128)S(1)}, f32[1024,256]{1,0:T(8,128)}, u32[]{:S(2)}) copy-start(f32[1024,256]{1,0:T(8,128)} %get-tuple-element.843) | copy-start | bytes 3145732
  4189.5 71.6 %copy-start.35 = (f32[256,1024]{1,0:T(8,128)S(1)}, f32[256,1024]{1,0:T(8,128)}, u32[]{:S(2)}) copy-start(f32[256,1024]{1,0:T(8,128)} %get-tuple-element.846) | copy-start | bytes 3145732
  4250.4 11.7 copy-start.30
  (57 other events, 331.5 us)
Sparse Core Ops, SparseCore 0:
  170.6 283.0 reduce-scatter.6
  455.3 287.4 all-gather.6
  843.7 278.4 reduce-scatter.8
  1123.7 287.4 all-gather.8
  1523.6 278.4 reduce-scatter.12
  1803.6 287.5 all-gather.12
  2223.6 278.4 reduce-scatter.14
  2503.6 287.4 all-gather.14
  2793.6 278.4 reduce-scatter.10
  3074.4 281.0 reduce-scatter.16
  3357.1 287.4 all-gather.10
  3652.0 221.1 all-reduce.6
  3874.8 287.8 all-gather.16
  4165.6 84.6 all-reduce.4
where the time goes:
time: 4290 us; the launch traced here: 4270 us
  waiting for transfers between devices  3210 us (75%)
  matrix products  495 us (12%)
  other arithmetic  291 us (7%)
  local copies, waits for them, and re-layouts  181 us (4%)
  blocking collectives  69.8 us (2%)
    all_gather x3, waiting for transfers between devices, add_branch(): lax.all_gather(branch_rows, 'mp', axis=0, tiled=True)  819 us
    all_gather x3, waiting for transfers between devices, norm_backward(): upstream = lax.all_gather(part_rows, 'mp', axis=0, tiled=True)  774 us
    reduce_scatter x3, waiting for transfers between devices, backward_rows(): return lax.psum_scatter(running, 'mp', scatter_dimension=0, tiled=True)  770 us
    reduce_scatter x3, waiting for transfers between devices, forward_rows(): lax.psum_scatter(jnp.dot(piece_rows, weight, preferred_element_type=jnp.f...  573 us
    psum x1, waiting for transfers between devices, on_device(): lax.psum((self_query_grad, self_key_grad, self_value_grad, self_out_grad,...  208 us
    dot_general x10, matrix products, right_product(): lax.dot_general(left_side, right_side, (((1,), (1,)), ((), ())), preferre...  119 us
  transfers between devices with their start and end apart: 14, of which 14 were waited for; matrix products, arithmetic and copies ran while one was open for 10% of the time, Pallas kernels for 0%

commit v1 on v0

v1 whole, which is shorter than its diff:
```python
import functools

import jax
import jax.numpy as jnp
from jax import lax
from jax.experimental import pallas as pl
from jax.experimental.pallas import tpu as pltpu
from jax.sharding import PartitionSpec as P

HEAD_DIM = 64
TXT = 128
SEQ = 1024
BLOCK = 256
WIDTH = 256
SCALING = HEAD_DIM ** (-0.5)
HIDDEN = -1e30
epsilon = 1e-05
bf16 = jnp.bfloat16
f32 = jnp.float32


def contract(left_side, right_side, left_dim, right_dim):
    return lax.dot_general(
        left_side, right_side, (((left_dim,), (right_dim,)), ((), ())), preferred_element_type=f32
    )


def head_masks(heads):
    column_head = lax.broadcasted_iota(jnp.int32, (1, heads * HEAD_DIM), 1) // HEAD_DIM
    return [(column_head == head).astype(f32).astype(bf16) for head in range(heads)]


def self_forward_kernel(query_ref, key_ref, value_ref, mixed_ref, sums_ref, turned_ref):
    seq_rows, width = query_ref.shape
    heads = width // HEAD_DIM
    block = min(BLOCK, seq_rows)
    masks = head_masks(heads)
    turned_ref[...] = value_ref[...].T
    key_pos = lax.broadcasted_iota(jnp.int32, (block, block), 0)
    query_pos = lax.broadcasted_iota(jnp.int32, (block, block), 1)
    allowed = key_pos <= query_pos
    for start in range(0, seq_rows, block):
        seen = start + block
        queries = query_ref[start:seen, :] * SCALING
        mixed = []
        for head in range(heads):
            scores = contract(key_ref[:seen, :], queries * masks[head], 1, 1)
            corner = jnp.where(allowed, scores[start:, :], HIDDEN)
            if start:
                scores = jnp.concatenate([scores[:start, :], corner], 0)
            else:
                scores = corner
            highest = jnp.max(scores, axis=0, keepdims=True)
            weights = jnp.exp(scores - highest)
            row_total = jnp.sum(weights, axis=0, keepdims=True)
            shares = (weights * (1.0 / row_total)).astype(bf16)
            rows = slice(head * HEAD_DIM, (head + 1) * HEAD_DIM)
            mixed.append(contract(turned_ref[rows, :seen], shares, 1, 0))
            sums_ref[head : head + 1, start:seen] = highest + jnp.log(row_total)
        mixed_ref[start:seen, :] = jnp.concatenate(mixed, 0).T.astype(bf16)


def self_backward_kernel(
    query_ref, key_ref, value_ref, grad_ref, sums_ref, dq_ref, dk_ref, dv_ref, turned_ref, dk_sum, dv_sum
):
    seq_rows, width = query_ref.shape
    heads = width // HEAD_DIM
    block = min(BLOCK, seq_rows)
    masks = head_masks(heads)
    turned_ref[...] = key_ref[...].T
    key_pos = lax.broadcasted_iota(jnp.int32, (block, block), 0)
    query_pos = lax.broadcasted_iota(jnp.int32, (block, block), 1)
    allowed = key_pos <= query_pos
    for start in range(seq_rows - block, -1, -block):
        seen = start + block
        queries = query_ref[start:seen, :] * SCALING
        grads = grad_ref[start:seen, :]
        query_parts, share_list, slope_list, query_list, grad_list = [], [], [], [], []
        for head in range(heads):
            one_query = queries * masks[head]
            one_grad = grads * masks[head]
            scores = contract(key_ref[:seen, :], one_query, 1, 1)
            corner = jnp.where(allowed, scores[start:, :], HIDDEN)
            if start:
                scores = jnp.concatenate([scores[:start, :], corner], 0)
            else:
                scores = corner
            shares = jnp.exp(scores - sums_ref[head : head + 1, start:seen])
            share_grad = contract(value_ref[:seen, :], one_grad, 1, 1)
            along = jnp.sum(shares * share_grad, axis=0, keepdims=True)
            slopes = (shares * (share_grad - along)).astype(bf16)
            rows = slice(head * HEAD_DIM, (head + 1) * HEAD_DIM)
            query_parts.append(contract(turned_ref[rows, :seen], slopes, 1, 0) * SCALING)
            share_list.append(shares.astype(bf16))
            slope_list.append(slopes)
            query_list.append(one_query)
            grad_list.append(one_grad)
        dq_ref[start:seen, :] = jnp.concatenate(query_parts, 0).T.astype(bf16)
        key_part = contract(jnp.concatenate(slope_list, 1), jnp.concatenate(query_list, 0), 1, 0)
        value_part = contract(jnp.concatenate(share_list, 1), jnp.concatenate(grad_list, 0), 1, 0)
        if seen == seq_rows:
            dk_sum[...] = key_part
            dv_sum[...] = value_part
        else:
            dk_sum[:seen, :] += key_part
            dv_sum[:seen, :] += value_part
    dk_ref[...] = dk_sum[...].astype(bf16)
    dv_ref[...] = dv_sum[...].astype(bf16)


def stack_heads(rows, masks):
    return jnp.concatenate([rows * mask for mask in masks], 0)


def cross_scores(stacked_keys, queries, length, heads):
    scores = contract(stacked_keys, queries * SCALING, 1, 1)
    slots = scores.shape[0] // heads
    inside = lax.broadcasted_iota(jnp.int32, (slots, scores.shape[1]), 0) < length
    return [
        jnp.where(inside, scores[head * slots : (head + 1) * slots, :], HIDDEN)
        for head in range(heads)
    ]


def cross_forward_kernel(lengths_ref, query_ref, key_ref, value_ref, mixed_ref, sums_ref):
    seq_rows, width = query_ref.shape
    heads = width // HEAD_DIM
    block = min(2 * BLOCK, seq_rows)
    masks = head_masks(heads)
    length = lengths_ref[pl.program_id(0)]
    stacked_keys = stack_heads(key_ref[...], masks)
    turned_values = stack_heads(value_ref[...], masks).T
    for start in range(0, seq_rows, block):
        queries = query_ref[start : start + block, :]
        shares = []
        for head, scores in enumerate(cross_scores(stacked_keys, queries, length, heads)):
            highest = jnp.max(scores, axis=0, keepdims=True)
            weights = jnp.exp(scores - highest)
            row_total = jnp.sum(weights, axis=0, keepdims=True)
            shares.append((weights * (1.0 / row_total)).astype(bf16))
            sums_ref[head : head + 1, start : start + block] = highest + jnp.log(row_total)
        mixed = contract(turned_values, jnp.concatenate(shares, 0), 1, 0)
        mixed_ref[start : start + block, :] = mixed.T.astype(bf16)


def cross_backward_kernel(
    lengths_ref, query_ref, key_ref, value_ref, grad_ref, sums_ref, dq_ref, dk_ref, dv_ref
):
    seq_rows, width = query_ref.shape
    heads = width // HEAD_DIM
    slots = key_ref.shape[0]
    block = min(2 * BLOCK, seq_rows)
    masks = head_masks(heads)
    length = lengths_ref[pl.program_id(0)]
    stacked_keys = stack_heads(key_ref[...], masks)
    stacked_values = stack_heads(value_ref[...], masks)
    turned_keys = stacked_keys.T
    key_sum, value_sum = None, None
    for start in range(0, seq_rows, block):
        queries = query_ref[start : start + block, :]
        grads = grad_ref[start : start + block, :]
        share_grads = contract(stacked_values, grads, 1, 1)
        share_list, slope_list = [], []
        for head, scores in enumerate(cross_scores(stacked_keys, queries, length, heads)):
            shares = jnp.exp(scores - sums_ref[head : head + 1, start : start + block])
            share_grad = share_grads[head * slots : (head + 1) * slots, :]
            along = jnp.sum(shares * share_grad, axis=0, keepdims=True)
            slope_list.append((shares * (share_grad - along)).astype(bf16))
            share_list.append(shares.astype(bf16))
        slopes = jnp.concatenate(slope_list, 0)
        query_part = contract(turned_keys, slopes, 1, 0) * SCALING
        dq_ref[start : start + block, :] = query_part.T.astype(bf16)
        key_part = contract(slopes, queries * SCALING, 1, 0)
        value_part = contract(jnp.concatenate(share_list, 0), grads, 1, 0)
        key_sum = key_part if key_sum is None else key_sum + key_part
        value_sum = value_part if value_sum is None else value_sum + value_part
    key_total, value_total = 0.0, 0.0
    for head in range(heads):
        mask = masks[head].astype(f32)
        key_total += key_sum[head * slots : (head + 1) * slots, :] * mask
        value_total += value_sum[head * slots : (head + 1) * slots, :] * mask
    dk_ref[...] = key_total.astype(bf16)
    dv_ref[...] = value_total.astype(bf16)


def block_spec(rows, width, first):
    return pl.BlockSpec((None, rows, width), lambda item, at, *_: (item, 0, first + at))


def sums_spec(heads, rows):
    return pl.BlockSpec((None, None, heads, rows), lambda item, at, *_: (item, at, 0, 0))


def kernel_params():
    return pltpu.CompilerParams(vmem_limit_bytes=48 * 1024 * 1024)


def self_forward(queries, key_rows, value_rows):
    items, rows, total = queries.shape
    width = min(WIDTH, total)
    blocks = total // width
    heads = width // HEAD_DIM
    return pl.pallas_call(
        self_forward_kernel,
        grid=(items, blocks),
        in_specs=[block_spec(rows, width, 0)] * 3,
        out_specs=[block_spec(rows, width, 0), sums_spec(heads, rows)],
        out_shape=[
            jax.ShapeDtypeStruct((items, rows, total), bf16),
            jax.ShapeDtypeStruct((items, blocks, heads, rows), f32),
        ],
        scratch_shapes=[pltpu.VMEM((width, rows), bf16)],
        compiler_params=kernel_params(),
        name="self_forward",
    )(queries, key_rows, value_rows)


def self_backward(queries, key_rows, value_rows, grads, sums_kept):
    items, rows, total = queries.shape
    width = min(WIDTH, total)
    blocks = total // width
    heads = width // HEAD_DIM
    return pl.pallas_call(
        self_backward_kernel,
        grid=(items, blocks),
        in_specs=[block_spec(rows, width, 0)] * 4 + [sums_spec(heads, rows)],
        out_specs=[block_spec(rows, width, 0)] * 3,
        out_shape=[jax.ShapeDtypeStruct((items, rows, total), bf16)] * 3,
        scratch_shapes=[
            pltpu.VMEM((width, rows), bf16),
            pltpu.VMEM((rows, width), f32),
            pltpu.VMEM((rows, width), f32),
        ],
        compiler_params=kernel_params(),
        name="self_backward",
    )(queries, key_rows, value_rows, grads, sums_kept)


def cross_forward(queries, key_rows, value_rows, lengths):
    items, rows, total = queries.shape
    slots = key_rows.shape[1]
    width = min(WIDTH, total)
    blocks = total // width
    heads = width // HEAD_DIM
    return pl.pallas_call(
        cross_forward_kernel,
        grid_spec=pltpu.PrefetchScalarGridSpec(
            num_scalar_prefetch=1,
            grid=(items, blocks),
            in_specs=[
                block_spec(rows, width, 0),
                block_spec(slots, width, 0),
                block_spec(slots, width, 0),
            ],
            out_specs=[block_spec(rows, width, 0), sums_spec(heads, rows)],
        ),
        out_shape=[
            jax.ShapeDtypeStruct(queries.shape, bf16),
            jax.ShapeDtypeStruct((items, blocks, heads, rows), f32),
        ],
        compiler_params=kernel_params(),
        name="cross_forward",
    )(lengths, queries, key_rows, value_rows)


def cross_backward(queries, key_rows, value_rows, lengths, grads, sums_kept):
    items, rows, total = queries.shape
    slots = key_rows.shape[1]
    width = min(WIDTH, total)
    blocks = total // width
    heads = width // HEAD_DIM
    return pl.pallas_call(
        cross_backward_kernel,
        grid_spec=pltpu.PrefetchScalarGridSpec(
            num_scalar_prefetch=1,
            grid=(items, blocks),
            in_specs=[
                block_spec(rows, width, 0),
                block_spec(slots, width, 0),
                block_spec(slots, width, 0),
                block_spec(rows, width, 0),
                sums_spec(heads, rows),
            ],
            out_specs=[
                block_spec(rows, width, 0),
                block_spec(slots, width, 0),
                block_spec(slots, width, 0),
            ],
        ),
        out_shape=[
            jax.ShapeDtypeStruct(queries.shape, bf16),
            jax.ShapeDtypeStruct((items, slots, total), bf16),
            jax.ShapeDtypeStruct((items, slots, total), bf16),
        ],
        compiler_params=kernel_params(),
        name="cross_backward",
    )(lengths, queries, key_rows, value_rows, grads, sums_kept)


def layer_stats(hidden):
    average = jnp.mean(hidden, axis=-1, keepdims=True)
    center = hidden - average
    variance = jnp.mean(center * center, axis=-1, keepdims=True)
    inverse = lax.rsqrt(variance + epsilon)
    return (center * inverse, inverse)


def norm_back(upstream, scaled, inverse, gain_vector):
    tilted = upstream * gain_vector
    return inverse * (
        tilted
        - jnp.mean(tilted, axis=-1, keepdims=True)
        - scaled * jnp.mean(tilted * scaled, axis=-1, keepdims=True)
    )


ROWS = 256
UNITS = 512


def row_block(rows, width):
    return pl.BlockSpec((rows, width), lambda at: (at, 0))


def whole_block(array):
    origin = (0,) * array.ndim
    return pl.BlockSpec(array.shape, lambda at: origin, pipeline_mode=pl.Buffered(1))


def unit_block(rows, width):
    return pl.BlockSpec((rows, width), lambda at: (0, at))


def line(vector):
    return vector.reshape(1, -1)


def shape_of(rows, width, dtype):
    return jax.ShapeDtypeStruct((rows, width), dtype)


class Gathered:
    def __init__(self, group, at, part):
        self.array = group
        self.at = at
        self.part = part
        self.shape = (group.shape[0] * group.shape[1] * part, group.shape[3])

    def spec(self):
        dp, mp, _, width = self.array.shape
        place = self.at
        return pl.BlockSpec(
            (dp, mp, self.part, width), lambda at: (0, 0, place, 0), pipeline_mode=pl.Buffered(1)
        )

    def put_in_order(self, part_ref, held_ref):
        dp, mp = self.array.shape[:2]
        for at_mp in range(mp):
            for at_dp in range(dp):
                start = (at_mp * dp + at_dp) * self.part
                held_ref[start : start + self.part, :] = part_ref[at_dp, at_mp]


def by_rows(body, name, row_ins, weights, vectors, outs, sums=0):
    rows, width = row_ins[0].shape[0], row_ins[-1].shape[1]
    block = min(ROWS, rows)
    vectors = [line(each) for each in vectors]
    counts = [len(row_ins), len(weights), len(vectors), len(outs) + (sums > 0)]

    def kernel(*refs):
        groups = []
        for count in counts:
            groups.append(refs[:count])
            refs = refs[count:]
        held = list(refs)
        ready = []
        for weight, ref in zip(weights, groups[1]):
            if isinstance(weight, Gathered):
                target = held.pop(0)
                pl.when(pl.program_id(0) == 0)(functools.partial(weight.put_in_order, ref, target))
                ref = target
            ready.append(ref)
        body(groups[0], ready, groups[2], groups[3])

    weight_specs, weight_arrays, scratch = [], [], []
    for weight in weights:
        if isinstance(weight, Gathered):
            weight_specs.append(weight.spec())
            weight_arrays.append(weight.array)
            scratch.append(pltpu.VMEM(weight.shape, bf16))
        else:
            weight_specs.append(whole_block(weight))
            weight_arrays.append(weight)
    out_specs = [row_block(block, each.shape[1]) for each in outs]
    out_shapes = list(outs)
    if sums:
        out_specs.append(pl.BlockSpec((sums, width), lambda at: (0, 0)))
        out_shapes.append(shape_of(sums, width, f32))
    return pl.pallas_call(
        kernel,
        grid=(rows // block,),
        in_specs=[row_block(block, each.shape[1]) for each in row_ins]
        + weight_specs
        + [whole_block(each) for each in vectors],
        out_specs=out_specs,
        out_shape=out_shapes,
        scratch_shapes=scratch,
        compiler_params=kernel_params(),
        name=name,
    )(*row_ins, *weight_arrays, *vectors)


def norm_project(hidden, gain, shift, weights):
    def body(rows, weight_refs, vectors, outs):
        scaled, _ = layer_stats(rows[0][...].astype(f32))
        normed = (scaled * vectors[0][...] + vectors[1][...]).astype(bf16)
        outs[0][...] = normed
        for weight_ref, out_ref in zip(weight_refs, outs[1:]):
            out_ref[...] = contract(normed, weight_ref[...], 1, 1).astype(bf16)

    rows, width = hidden.shape
    outs = [shape_of(rows, width, bf16)] + [shape_of(rows, each.shape[0], bf16) for each in weights]
    return by_rows(body, "norm_project", [hidden], weights, [gain, shift], outs)


def add_branch(mixed, weight, before, add, gain, shift, following):
    def body(rows, weight_refs, vectors, outs):
        branch = contract(rows[0][...], weight_refs[0][...], 1, 0) + vectors[0][...]
        hidden = rows[1][...].astype(f32) + branch
        scaled, _ = layer_stats(hidden)
        normed = (scaled * vectors[1][...] + vectors[2][...]).astype(bf16)
        outs[0][...] = hidden
        outs[1][...] = normed
        for weight_ref, out_ref in zip(weight_refs[1:], outs[2:]):
            out_ref[...] = contract(normed, weight_ref[...], 1, 1).astype(bf16)

    rows, width = before.shape
    outs = [shape_of(rows, width, f32), shape_of(rows, width, bf16)]
    outs += [shape_of(rows, each.shape[0], bf16) for each in following]
    return by_rows(
        body, "add_branch", [mixed, before], [weight, *following], [add, gain, shift], outs
    )


def products(left, weights):
    def body(rows, weight_refs, vectors, outs):
        for weight_ref, out_ref in zip(weight_refs, outs):
            out_ref[...] = contract(rows[0][...], weight_ref[...], 1, 1).astype(bf16)

    outs = [shape_of(left.shape[0], each.shape[0], bf16) for each in weights]
    return by_rows(body, "products", [left], weights, [], outs)


def side_sum(sides, weights):
    total = contract(sides[0][...], weights[0][...], 1, 0)
    for side, weight in zip(sides[1:], weights[1:]):
        total = total + contract(side[...], weight[...], 1, 0)
    return total


def sum_products(sides, weights):
    def body(rows, weight_refs, vectors, outs):
        outs[0][...] = side_sum(rows, weight_refs).astype(bf16)

    outs = [shape_of(sides[0].shape[0], weights[0].shape[1], bf16)]
    return by_rows(body, "sum_products", sides, weights, [], outs)[0]


def layer_output(near, far, near_weight, far_weight, before, add):
    mp, chips, part, width = near_weight.shape

    def body(rows, weight_refs, vectors, outs):
        total = rows[2][...] + vectors[0][...]
        for side, weight in zip(rows[:2], weight_refs):
            for at in range(chips):
                columns = side[:, at * mp * part : (at + 1) * mp * part]
                total = total + contract(columns, weight[:, at].reshape(mp * part, width), 1, 0)
        outs[0][...] = total.astype(bf16)

    outs = [shape_of(*before.shape, bf16)]
    return by_rows(
        body, "layer_output", [near, far, before], [near_weight, far_weight], [add], outs
    )[0]


def norm_grad(sides, weights, hidden, above, gain, following):
    count = len(sides)

    def body(rows, weight_refs, vectors, outs):
        upstream = side_sum(rows[:count], weight_refs[:count])
        scaled, inverse = layer_stats(rows[count][...].astype(f32))
        above_rows = rows[count + 1][...].astype(f32)
        grad = above_rows + norm_back(upstream, scaled, inverse, vectors[0][...])
        low = grad.astype(bf16)
        outs[0][...] = low
        if following is not None:
            outs[1][...] = grad
            outs[2][...] = contract(low, weight_refs[count][...], 1, 1).astype(bf16)
        sums_ref = outs[-1]

        @pl.when(pl.program_id(0) == 0)
        def _():
            sums_ref[...] = jnp.zeros_like(sums_ref)

        for at, each in enumerate([upstream * scaled, upstream, low.astype(f32), above_rows]):
            sums_ref[at : at + 1, :] += jnp.sum(each, axis=0, keepdims=True)

    rows, width = hidden.shape
    outs = [shape_of(rows, width, bf16)]
    if following is not None:
        weights = [*weights, following]
        outs += [shape_of(rows, width, f32), shape_of(rows, following.shape[0], bf16)]
    return by_rows(body, "norm_grad", [*sides, hidden, above], weights, [gain], outs, sums=8)


def units_kernel(normed_ref, weight_ref, bias_ref, active_ref, slope_ref):
    rows = normed_ref.shape[0]
    block = min(ROWS, rows)
    for start in range(0, rows, block):
        at = slice(start, start + block)
        inner = contract(normed_ref[at, :], weight_ref[...], 1, 1) + bias_ref[...]
        below = 0.5 * (1.0 + lax.erf(inner * (0.5**0.5)))
        slope = below + inner * (jnp.exp(-0.5 * inner * inner) * 0.3989422804014327)
        active_ref[at, :] = (inner * below).astype(bf16)
        slope_ref[at, :] = slope.astype(bf16)


def hidden_units(normed, weight, bias):
    rows, width = normed.shape
    units = weight.shape[0]
    block = min(UNITS, units)
    return pl.pallas_call(
        units_kernel,
        grid=(units // block,),
        in_specs=[whole_block(normed), row_block(block, width), unit_block(1, block)],
        out_specs=[unit_block(rows, block)] * 2,
        out_shape=[shape_of(rows, units, bf16)] * 2,
        compiler_params=kernel_params(),
        name="hidden_units",
    )(normed, weight, line(bias))


def units_grad_kernel(
    active_ref, slope_ref, weight_ref, top_ref, normed_ref, inner_ref, out_ref, in_ref, sums_ref
):
    top = top_ref[...]
    out_ref[...] = contract(active_ref[...], top, 0, 0).astype(bf16)
    weight = weight_ref[...].reshape(-1, top.shape[1])
    inner = contract(top, weight, 1, 1) * slope_ref[...].astype(f32)
    inner = inner.astype(bf16)
    inner_ref[...] = inner
    sums_ref[...] = jnp.sum(inner.astype(f32), axis=0, keepdims=True)
    in_ref[...] = contract(inner, normed_ref[...], 0, 0).astype(bf16)


def units_grad(active, slope, weight, top, normed):
    rows, width = top.shape
    mp, chips, part = weight.shape[:3]
    units, block = mp * chips * part, mp * part
    return pl.pallas_call(
        units_grad_kernel,
        grid=(units // block,),
        in_specs=[unit_block(rows, block)] * 2
        + [
            pl.BlockSpec((mp, None, part, width), lambda at: (0, at, 0, 0)),
            whole_block(top),
            whole_block(normed),
        ],
        out_specs=[
            unit_block(rows, block),
            row_block(block, width),
            row_block(block, width),
            unit_block(1, block),
        ],
        out_shape=[
            shape_of(rows, units, bf16),
            shape_of(units, width, bf16),
            shape_of(units, width, bf16),
            shape_of(1, units, f32),
        ],
        compiler_params=kernel_params(),
        name="units_grad",
    )(active, slope, weight, top, normed)


def deal_kernel(mp, dp, own_ref, *refs):
    operands, outs = refs[: 2 * len(refs) // 3], refs[2 * len(refs) // 3 :]
    core, chip = own_ref[0] % 2, own_ref[0] // 2
    for at in range(len(operands) // 2):
        near_ref, far_ref = outs[at // 2 * 2], outs[at // 2 * 2 + 1]
        product = contract(operands[2 * at][...], operands[2 * at + 1][...], 0, 0).astype(bf16)
        part = product.shape[0] // (mp * dp)
        for at_mp in range(mp):
            for at_chip in range(dp // 2):
                start = (at_mp * dp + 2 * at_chip) * part
                even = product[start : start + part, :]
                odd = product[start + part : start + 2 * part, :]
                place = at_chip ^ chip
                near_ref[place, at_mp, at % 2] = jnp.where(core == 0, even, odd)
                far_ref[place, at_mp, at % 2] = jnp.where(core == 0, odd, even)


def deal_grads(*factors):
    mp, dp = lax.axis_size("mp"), lax.axis_size("dp")
    features, width = factors[0][0].shape[1], factors[0][1].shape[1]
    shape = (dp // 2, mp, 2, features // (mp * dp), width)
    operands = [each for pair in factors for each in pair]
    once = pl.Buffered(1)
    return pl.pallas_call(
        functools.partial(deal_kernel, mp, dp),
        grid_spec=pltpu.PrefetchScalarGridSpec(
            num_scalar_prefetch=1,
            grid=(1,),
            in_specs=[
                pl.BlockSpec(each.shape, lambda at, own: (0, 0), pipeline_mode=once)
                for each in operands
            ],
            out_specs=[
                pl.BlockSpec(shape, lambda at, own: (0, 0, 0, 0, 0), pipeline_mode=once)
                for _ in factors
            ],
        ),
        out_shape=[jax.ShapeDtypeStruct(shape, bf16) for _ in factors],
        compiler_params=kernel_params(),
        name="deal_grads",
    )(lax.axis_index("dp").reshape(1), *operands)


def column_part(shard):
    share = shard.shape[1] // lax.axis_size("dp")
    return lax.dynamic_slice_in_dim(shard, lax.axis_index("dp") * share, share, 1).T


def row_part(shard):
    share = shard.shape[0] // lax.axis_size("dp")
    return lax.dynamic_slice_in_dim(shard, lax.axis_index("dp") * share, share, 0)


def swap(value, axis, mask):
    count = lax.axis_size(axis)
    return lax.ppermute(value, axis, [(at, at ^ mask) for at in range(count)])


def chip_masks():
    return list(range(2, lax.axis_size("dp"), 2))


def tie(value, *others):
    anywhere = pl.BlockSpec(memory_space=pl.ANY)
    return pl.pallas_call(
        lambda *refs: None,
        in_specs=[anywhere] * (1 + len(others)),
        out_specs=anywhere,
        out_shape=jax.ShapeDtypeStruct(value.shape, value.dtype),
        input_output_aliases={0: 0},
        name="tie",
    )(value, *others)


def tie_all(values, *others):
    anywhere = pl.BlockSpec(memory_space=pl.ANY)
    return pl.pallas_call(
        lambda *refs: None,
        in_specs=[anywhere] * (len(values) + len(others)),
        out_specs=[anywhere] * len(values),
        out_shape=[jax.ShapeDtypeStruct(each.shape, each.dtype) for each in values],
        input_output_aliases={at: at for at in range(len(values))},
        name="tie_all",
    )(*values, *others)


def arrived(values, after):
    return tie_all(values, *after) if after else values


def gather_mp(value, axis=0, after=()):
    pieces = [swap(value, "mp", mask) for mask in range(1, lax.axis_size("mp"))]
    return jnp.stack([value, *arrived(pieces, after)], axis)


def low_sum(*terms):
    total = terms[0].astype(f32)
    for term in terms[1:]:
        total = total + term.astype(f32)
    return total.astype(bf16)


class PairSum:
    def __init__(self, terms, axis, unit, up):
        self.axis, self.unit = axis, unit
        count = terms[0].shape[0]
        bits = [1 << at for at in range(count.bit_length() - 1)]
        self.left = bits[::-1]
        self.order = bits if up else bits[::-1]
        self.terms = [each.reshape((2,) * len(bits) + each.shape[1:]) for each in terms]

    def step(self, after=()):
        bit, *self.order = self.order
        place = self.left.index(bit)
        self.left.remove(bit)
        sent = low_sum(*[lax.index_in_dim(each, 1, place, keepdims=False) for each in self.terms])
        [taken] = arrived([swap(sent, self.axis, self.unit * bit)], after)
        kept = [lax.index_in_dim(each, 0, place, keepdims=False) for each in self.terms]
        self.terms = kept + [taken]
        return taken

    def total(self, after=()):
        while self.order:
            self.step(after)
        return low_sum(*self.terms)


class PlaneSum(PairSum):
    def __init__(self, near, far, up):
        self.near, self.far, self.up = near, far, up

    def core(self, after=()):
        [taken] = arrived([swap(self.far, "dp", 1)], after)
        super().__init__([self.near, taken], "dp", 2, self.up)
        return taken

    def total(self, after=()):
        summed = super().total(after)
        return summed.reshape(summed.shape[0], -1, summed.shape[-1])


def over_mp(pieces):
    return PairSum([pieces], "mp", 1, True)


def spread(part, after=(), after_core=()):
    taken = [swap(part, "dp", mask) for mask in chip_masks()]
    near = jnp.stack([part, *arrived(taken, after)], 0)
    return jnp.concatenate([near, *arrived([swap(near, "dp", 1)], after_core)], 0)


def places_of_dp():
    apart = jnp.arange(lax.axis_size("dp"), dtype=jnp.int32) ^ lax.axis_index("dp")
    return (apart % 2) * (lax.axis_size("dp") // 2) + apart // 2


def settle_kernel(from_ref, *refs):
    refs[-1][...] = from_ref[...]


def settle(gathered, at, count, into=None):
    rows, width = gathered.shape
    block = rows // lax.axis_size("mp")
    before = [] if into is None else [into]
    return pl.pallas_call(
        settle_kernel,
        grid=(rows // block,),
        in_specs=[row_block(block, width)] + [pl.BlockSpec(memory_space=pl.ANY)] * len(before),
        out_specs=pl.BlockSpec((block, width), lambda step: (step * count + at, 0)),
        out_shape=shape_of(rows * count, width, gathered.dtype),
        input_output_aliases={1: 0} if before else {},
        compiler_params=kernel_params(),
        name="settle",
    )(gathered, *before)


def place_kernel(places_ref, part_ref, whole_ref):
    whole_ref[...] = part_ref[...].astype(f32)


def place(pieces, places):
    count, rows, width = pieces.shape
    return pl.pallas_call(
        place_kernel,
        grid_spec=pltpu.PrefetchScalarGridSpec(
            num_scalar_prefetch=1,
            grid=(count,),
            in_specs=[pl.BlockSpec((None, rows, width), lambda at, places: (places[at], 0, 0))],
            out_specs=pl.BlockSpec((rows, width), lambda at, places: (at, 0)),
        ),
        out_shape=shape_of(count * rows, width, f32),
        compiler_params=kernel_params(),
        name="place",
    )(places, pieces)


def finish_kernel(turned, places_ref, part_ref, whole_ref):
    count = part_ref.shape[0]
    rows = jnp.concatenate([part_ref[places_ref[at]] for at in range(count)], 0).astype(f32)
    whole_ref[...] = rows.T if turned else rows


def finish(value, places, first, rows, turned):
    count, total, width = value.shape
    value = value.reshape(count, total // rows, rows, width)
    at = first // rows
    shape = (width, count * rows) if turned else (count * rows, width)
    return pl.pallas_call(
        functools.partial(finish_kernel, turned),
        grid_spec=pltpu.PrefetchScalarGridSpec(
            num_scalar_prefetch=1,
            grid=(1,),
            in_specs=[pl.BlockSpec((count, None, rows, width), lambda i, places: (0, at, 0, 0))],
            out_specs=pl.BlockSpec(shape, lambda i, places: (0, 0)),
        ),
        out_shape=jax.ShapeDtypeStruct(shape, f32),
        compiler_params=kernel_params(),
        name="finish",
    )(places, value)


def on_device(
    inputs,
    text_states,
    text_lengths,
    norm1_gain,
    norm1_bias,
    self_query,
    self_key,
    self_value,
    self_out,
    self_out_bias,
    norm2_gain,
    norm2_bias,
    cross_query,
    cross_key,
    cross_value,
    cross_out,
    cross_out_bias,
    norm3_gain,
    norm3_bias,
    mlp_in,
    mlp_in_bias,
    mlp_out,
    mlp_out_bias,
    cotangent,
):
    mp, dp = lax.axis_size("mp"), lax.axis_size("dp")
    at_mp = lax.axis_index("mp")
    items_here = text_states.shape[0]
    width = inputs.shape[1]
    copies = max(1, mp // items_here)
    own_items = max(1, items_here // mp)
    first_item = (at_mp // copies) * own_items
    own_rows = own_items * SEQ

    def own(whole, count):
        return lax.dynamic_slice_in_dim(whole, first_item * count, own_items * count, 0)

    def counted(value):
        if copies == 1:
            return value
        return value * (at_mp % copies == 0).astype(value.dtype)

    def share_of(local):
        if copies == 1:
            return local
        part = local.shape[0] // copies
        return lax.dynamic_slice_in_dim(local, (at_mp % copies) * part, part, 0)

    def share_halves(local):
        local = share_of(local)
        half_rows = local.shape[0] // 2
        return [
            lax.all_gather(local[at * half_rows : (at + 1) * half_rows], "mp", axis=0, tiled=True)
            for at in range(2)
        ]

    def by_item(rows):
        return rows.reshape(own_items, -1, rows.shape[-1])

    part_of = self_query.shape[1] // dp
    hidden_part = mlp_in.shape[1] // dp
    at_dp = lax.axis_index("dp")
    near_indices = jnp.asarray([0] + chip_masks(), jnp.int32) ^ at_dp
    parts = jnp.concatenate([column_part(self_query), column_part(self_key), column_part(self_value)], 0)
    over_mp_self = gather_mp(parts)
    parts = jnp.concatenate(
        [
            tie(row_part(self_out), over_mp_self),
            column_part(cross_query),
            column_part(cross_key),
            column_part(cross_value),
            row_part(cross_out),
        ],
        0,
    )
    over_mp_cross = gather_mp(parts)
    self_group = lax.all_gather(over_mp_self, "dp", axis=0, tiled=False)
    self_weights = [Gathered(self_group, at, part_of) for at in range(3)]
    half = jnp.concatenate(
        [
            lax.dynamic_slice_in_dim(mlp_out, (at_dp ^ mask) * hidden_part, hidden_part, 0)[None]
            for mask in [0] + chip_masks()
        ],
        0,
    )

    tokens = own(inputs, SEQ)
    lengths = own(text_lengths, 1)
    texts = own(text_states, 1).reshape(own_items * TXT, width)
    grad_top = own(cotangent, SEQ)
    bias_whole = gather_mp(mlp_in_bias)
    gain = tie(norm1_gain, bias_whole)
    normed_self, *projected = norm_project(tokens, gain, norm1_bias, self_weights)
    cross_group = lax.all_gather(over_mp_cross, "dp", axis=0, tiled=False)
    self_out_whole, cross_query_whole, cross_key_whole, cross_value_whole, cross_out_whole = [
        Gathered(cross_group, at, part_of) for at in range(5)
    ]
    projected = [by_item(each) for each in projected]
    over_mp_in = gather_mp(tie(column_part(mlp_in), over_mp_cross), 0, [normed_self])
    half = tie(half, normed_self)
    self_mixed, self_sums = self_forward(*projected)
    mixed_rows = self_mixed.reshape(own_rows, width)
    over_mp_in = tie(over_mp_in, self_mixed)
    in_pieces = [swap(over_mp_in, "dp", mask) for mask in chip_masks()]
    hidden_one, normed_cross, cross_queries = add_branch(
        mixed_rows, self_out_whole, tokens, self_out_bias, norm2_gain, norm2_bias, [cross_query_whole]
    )
    cross_queries = by_item(cross_queries)
    cross_keys, cross_values = products(texts, [cross_key_whole, cross_value_whole])
    cross_keys, cross_values = by_item(cross_keys), by_item(cross_values)
    cross_mixed, cross_sums = cross_forward(cross_queries, cross_keys, cross_values, lengths)
    cross_rows = cross_mixed.reshape(own_rows, width)
    in_near = jnp.stack([over_mp_in, *tie_all(in_pieces, cross_mixed)], 0)
    in_far = swap(in_near, "dp", 1).reshape(-1, width)
    in_near = in_near.reshape(-1, width)
    hidden_two, normed_mlp = add_branch(
        cross_rows, cross_out_whole, hidden_one, cross_out_bias, norm3_gain, norm3_bias, []
    )
    bias_whole = bias_whole.reshape(mp, dp, hidden_part)
    bias_near = jnp.swapaxes(bias_whole[:, near_indices], 0, 1).reshape(-1)
    bias_far = jnp.swapaxes(bias_whole[:, near_indices ^ 1], 0, 1).reshape(-1)
    active_near, slope_near = hidden_units(normed_mlp, in_near, bias_near)
    out_near = gather_mp(half, 0, [active_near])
    out_far = swap(out_near, "dp", 1)
    active_far, slope_far = hidden_units(normed_mlp, in_far, bias_far)

    output = layer_output(active_near, active_far, out_near, out_far, hidden_two, mlp_out_bias)
    slope_far = tie(slope_far, output)
    output_halves = share_halves(output)
    inner_far, *far_parts, far_sums = units_grad(active_far, slope_far, out_far, grad_top, normed_mlp)
    inner_near, *near_parts, near_sums = units_grad(active_near, slope_near, out_near, grad_top, normed_mlp)

    def units_sum(which, up):
        halves = [
            counted(each[which]).reshape(dp // 2, mp, hidden_part, width)
            for each in (near_parts, far_parts)
        ]
        return PlaneSum(*halves, up)

    out_sum, in_sum = units_sum(0, True), units_sum(1, False)
    gain = tie(norm3_gain, out_sum.core([near_sums]), in_sum.core([near_sums]))
    branch_grad, hidden_two_grad, mixed_grad, sums_three = norm_grad(
        [inner_near, inner_far], [in_near, in_far], hidden_two, grad_top, gain, cross_out_whole
    )
    cross_sums = tie(cross_sums, out_sum.step([sums_three]), in_sum.step([sums_three]))
    query_grad, key_grad, value_grad = cross_backward(
        cross_queries, cross_keys, cross_values, lengths, by_item(mixed_grad), cross_sums
    )
    query_grad = query_grad.reshape(own_rows, width)
    key_grad = key_grad.reshape(own_items * TXT, width)
    value_grad = value_grad.reshape(own_items * TXT, width)

    def dealt_sums(*factors):
        near_a, far_a, near_b, far_b = [counted(each) for each in deal_grads(*factors)]
        return PlaneSum(near_a, far_a, True), PlaneSum(near_b, far_b, False)

    cross_a, cross_b = dealt_sums(
        (cross_rows, branch_grad), (query_grad, normed_cross), (key_grad, texts), (value_grad, texts)
    )
    text_grad = sum_products([key_grad, value_grad], [cross_key_whole, cross_value_whole])
    dealt = [cross_a.far]
    mlp_total = jnp.concatenate([out_sum.total(dealt), in_sum.total(dealt)], 1)
    gain = tie(norm2_gain, mlp_total, text_grad, output_halves[0])
    output = settle(output_halves[0], 0, 2)
    branch_grad, hidden_one_grad, mixed_grad, sums_two = norm_grad(
        [query_grad], [cross_query_whole], hidden_one, hidden_two_grad, gain, self_out_whole
    )
    text_sides = swap(share_of(text_grad)[None], "mp", mp // 2)
    text_sides = jnp.concatenate([share_of(text_grad)[None], *arrived([text_sides], [sums_two])], 0)
    self_sums = tie(self_sums, text_sides, cross_a.core([sums_two]), cross_b.core([sums_two]))
    side_grads = self_backward(*projected, by_item(mixed_grad), self_sums)
    side_grads = [each.reshape(own_rows, width) for each in side_grads]
    side = [side_grads[0]]
    mlp_sum = over_mp(mlp_total)
    bits = [mp // 2]
    while bits[-1] > 1:
        bits.append(bits[-1] // 2)
        text_sides = jnp.concatenate([text_sides, *arrived([swap(text_sides, "mp", bits[-1])], side)], 0)
    output = settle(output_halves[1], 1, 2, output)
    gain = tie(norm1_gain, output_halves[1], cross_a.step(side), cross_b.step(side), mlp_sum.step(side), text_sides)
    input_grad, sums_one = norm_grad(side_grads, self_weights, tokens, hidden_one_grad, gain, None)
    input_halves = share_halves(input_grad)
    input_grad = settle(input_halves[0], 0, 2)
    input_start = input_grad[:8, :128]
    input_grad = settle(input_halves[1], 1, 2, input_grad)
    mp_places = jnp.arange(mp, dtype=jnp.int32) ^ at_mp
    text_places = sum(((mp_places // bit) % 2) << at for at, bit in enumerate(bits))
    text_grad = place(text_sides, text_places)

    normed = [sums_one]
    cross_total = jnp.concatenate([cross_a.total(normed), cross_b.total(normed)], 1)
    mlp_part = mlp_sum.total(normed)
    value_side = tie(side_grads[2], sums_one, cross_total, mlp_part)
    self_a, self_b = dealt_sums(
        (side_grads[0], normed_self),
        (side_grads[1], normed_self),
        (value_side, normed_self),
        (mixed_rows, branch_grad),
    )
    dealt = [self_a.near]
    cross_part = over_mp(cross_total).total(dealt)
    mlp_parts = spread(mlp_part, dealt)
    self_a.core()
    self_b.core()
    self_total = jnp.concatenate([self_a.total(), self_b.total()], 1)
    cross_parts = spread(cross_part)
    late = spread(over_mp(self_total).total())
    places = places_of_dp()
    late_places = tie(places, input_start)
    mlp_out_grad = finish(mlp_parts, places, 0, hidden_part, False)
    mlp_in_grad = finish(mlp_parts, places, hidden_part, hidden_part, True)
    cross_out_grad, cross_query_grad, cross_key_grad, cross_value_grad = [
        finish(cross_parts, places, at * part_of, part_of, at > 0) for at in range(4)
    ]
    self_query_grad, self_key_grad, self_value_grad, self_out_grad = [
        finish(late, late_places, at * part_of, part_of, at < 3) for at in range(4)
    ]

    inner_sums = jnp.concatenate([near_sums, far_sums], 0).reshape(dp, mp, hidden_part)
    inner_sums = jnp.swapaxes(inner_sums[places][:, mp_places], 0, 1).reshape(-1, width)
    vectors = [sums_three[3], sums_three[0], sums_three[1], sums_three[2], sums_two[0], sums_two[1]]
    vectors += [sums_two[2], sums_one[0], sums_one[1]]
    sums = counted(jnp.concatenate([jnp.stack(vectors), inner_sums], 0))
    for axis, count in (("mp", mp), ("dp", dp)):
        reach = 1
        while reach < count:
            sums = sums + swap(sums, axis, reach)
            reach *= 2
    units_here = mlp_in_bias.shape[0]
    mlp_in_bias_grad = lax.dynamic_slice_in_dim(
        sums[len(vectors) :].reshape(-1), at_mp * units_here, units_here, 0
    )
    return (
        output,
        input_grad,
        text_grad.reshape(text_states.shape),
        sums[7],
        sums[8],
        self_query_grad,
        self_key_grad,
        self_value_grad,
        self_out_grad,
        sums[6],
        sums[4],
        sums[5],
        cross_query_grad,
        cross_key_grad,
        cross_value_grad,
        cross_out_grad,
        sums[3],
        sums[1],
        sums[2],
        mlp_in_grad,
        mlp_in_bias_grad,
        mlp_out_grad,
        sums[0],
    )


def solution(mesh):
    rows, column, row, everywhere = P("dp", None), P(None, "mp"), P("mp", None), P()
    return jax.shard_map(
        on_device,
        mesh=mesh,
        in_specs=(
            rows,
            P("dp", None, None),
            P("dp"),
            everywhere,
            everywhere,
            column,
            column,
            column,
            row,
            everywhere,
            everywhere,
            everywhere,
            column,
            column,
            column,
            row,
            everywhere,
            everywhere,
            everywhere,
            column,
            P("mp"),
            row,
            everywhere,
            rows,
        ),
        out_specs=(
            rows,
            rows,
            P("dp", None, None),
            everywhere,
            everywhere,
            column,
            column,
            column,
            row,
            everywhere,
            everywhere,
            everywhere,
            column,
            column,
            column,
            row,
            everywhere,
            everywhere,
            everywhere,
            column,
            P("mp"),
            row,
            everywhere,
        ),
        check_vma=False,
    )
```

time: 4290 us -> 793 us (0.18)
  waiting for transfers between devices: 3210 us -> 220 us
  matrix products: 495 us -> 0 us
  Pallas kernels: 0 us -> 312 us
  other arithmetic: 291 us -> 79.6 us
  local copies, waits for them, and re-layouts: 181 us -> 83.7 us
  starting transfers between devices: 0.56 us -> 75.9 us
  blocking collectives: 69.8 us -> 0 us
    all_gather x6, waiting for transfers between devices: 1590 us -> 0.06 us  [the longest x4 0.05 us: share_halves(): lax.all_gather(local[at * half_rows:(at + 1) * half_rows], 'mp', axis=0,...]
    reduce_scatter x6 -> x0, waiting for transfers between devices: 1340 us -> none  [the longest x3 770 us: backward_rows(): return lax.psum_scatter(running, 'mp', scatter_dimension=0, tiled=True)]
    dot_general x142 -> x0, matrix products: 495 us -> none  [the longest x10 119 us: right_product(): lax.dot_general(left_side, right_side, (((1,), (1,)), ((), ())), preferre...]
    pallas_call x0 -> x69, Pallas kernels: none -> 312 us  [the longest x9 99.4 us: by_rows(): pl.pallas_call(kernel, grid=(rows // block,), in_specs=[row_block(block,...]
    psum x2 -> x0, waiting for transfers between devices: 269 us -> none  [the longest x1 208 us: on_device(): lax.psum((self_query_grad, self_key_grad, self_value_grad, self_out_grad,...]
    ppermute x0 -> x63, waiting for transfers between devices: none -> 220 us  [swap(): return lax.ppermute(value, axis, [(at, at ^ mask) for at in range(count)])]
    reduce_sum x31 -> x0, other arithmetic: 116 us -> none  [the longest x3 36.7 us: norm_back(): jnp.mean(tilted, axis=-1, keepdims=True)]
    ppermute x0 -> x63, starting transfers between devices: none -> 75.6 us  [swap(): return lax.ppermute(value, axis, [(at, at ^ mask) for at in range(count)])]
  transfers between devices with their start and end apart: 14 -> 69, of which waited for: 14 -> 21; matrix products, arithmetic and copies ran while one was open for 10% -> 14% of each run, Pallas kernels for 0% -> 35%
where the time goes in v1:
time: 793 us; the launch traced here: 787 us
  Pallas kernels  312 us (39%)
  waiting for transfers between devices  220 us (28%)
  local copies, waits for them, and re-layouts  83.7 us (11%)
  other arithmetic  79.6 us (10%)
  starting transfers between devices  75.9 us (10%)
  between operations  15.5 us (2%)
    ppermute x63, waiting for transfers between devices, swap(): return lax.ppermute(value, axis, [(at, at ^ mask) for at in range(count)])  220 us
    pallas_call x9, Pallas kernels, by_rows(): pl.pallas_call(kernel, grid=(rows // block,), in_specs=[row_block(block,...  99.4 us
    ppermute x63, starting transfers between devices, swap(): return lax.ppermute(value, axis, [(at, at ^ mask) for at in range(count)])  75.6 us
    convert_element_type x24, other arithmetic, low_sum(): return total.astype(bf16)  56.6 us
    unnamed x218, local copies, waits for them, and re-layouts  54.5 us
    pallas_call x1, Pallas kernels, self_backward(): pl.pallas_call(self_backward_kernel, grid=(items, blocks), in_specs=[bloc...  47 us
    pallas_call x2, Pallas kernels, units_grad(): pl.pallas_call(units_grad_kernel, grid=(units // block,), in_specs=[unit_...  34.4 us
    pallas_call x1, Pallas kernels, self_forward(): pl.pallas_call(self_forward_kernel, grid=(items, blocks), in_specs=[block...  29.9 us
  transfers between devices with their start and end apart: 69, of which 21 were waited for; matrix products, arithmetic and copies ran while one was open for 14% of the time, Pallas kernels for 35%

profile of v1, /device:TPU:0, one launch (start us, length us, event | category | flops | bytes accessed | tf_op | source)
XLA Modules:
  0.0 787.0 jit_solution(13673255598465067817)
XLA Ops:
  12.4 3.1 collective-permute-start
  15.5 2.6 collective-permute-start.1
  18.1 5.7 collective-permute-done
  23.9 8.8 %collective-permute-done.1 = bf16[96,1024]{1,0:T(8,128)(2,1)S(1)} collective-permute-done((bf16[96,1024]{1,0:T(8,128)(2,1)S(1)}, bf16[96,1024]{1,0:T(8,128)(2,1)S(1)}, u32[]{:S(2)}, u32[]{:S(2)}) %collective-permute-start.1) | collective-permute-done | bytes 196640 | tf_op jit(solution)/shard_map/ppermute | solution.py:641
  38.5 3.4 collective-permute-start.6
  44.4 9.8 %collective-permute-done.6 = bf16[160,1024]{1,0:T(8,128)(2,1)S(1)} collective-permute-done((bf16[160,1024]{1,0:T(8,128)(2,1)S(1)}, bf16[160,1024]{1,0:T(8,128)(2,1)S(1)}, u32[]{:S(2)}, u32[]{:S(2)}) %collective-permute-start.6) | collective-permute-done | bytes 327712 | tf_op jit(solution)/shard_map/ppermute | solution.py:641
  54.1 13.4 %collective-permute-done.7 = bf16[160,1024]{1,0:T(8,128)(2,1)S(1)} collective-permute-done((bf16[160,1024]{1,0:T(8,128)(2,1)S(1)}, bf16[160,1024]{1,0:T(8,128)(2,1)S(1)}, u32[]{:S(2)}, u32[]{:S(2)}) %collective-permute-start.7) | collective-permute-done | bytes 327712 | tf_op jit(solution)/shard_map/ppermute | solution.py:641
  68.8 6.1 collective-permute-start.4
  77.1 3.0 collective-permute-start.10
  81.5 3.1 constant_dynamic-slice_fusion.9.refs_0_.refs_1_.refs_3_
  86.5 12.9 %norm_project.1 = (bf16[1024,1024]{1,0:T(8,128)(2,1)S(1)}, bf16[1024,1024]{1,0:T(8,128)(2,1)S(1)}, bf16[1024,1024]{1,0:T(8,128)(2,1)}, bf16[1024,1024]{1,0:T(8,128)(2,1)}) custom-call(bf16[1024,1024]{1,0:T(8,128)(2,1)} %constant_dynamic-slice_fusion.9.refs_0_.refs_1_.refs_3_, bf16[8,4,96,1024]{3,2,1,0:T(8,128)(2,1)} %bitcast.368, ...), custom_call_target="tpu_custom_call" | custom-call | tf_op jit(solution)/shard_map/norm_project/pallas_call | solution.py:399
  100.8 29.9 %self_forward.1 = (bf16[1,1024,1024]{2,1,0:T(8,128)(2,1)S(1)}, f32[1,4,4,1024]{3,2,1,0:T(4,128)S(1)}) custom-call(bf16[1,1024,1024]{2,1,0:T(8,128)(2,1)S(1)} %bitcast.329, bf16[1,1024,1024]{2,1,0:T(8,128)(2,1)} %bitcast.396, bf16[1,1024,1024]{2,1,0:T(8,128)(2,1)} %bitcast.398), custom_call_target="tpu_custom_call" | custom-call | tf_op jit(solution)/shard_map/self_forward/pallas_call | solution.py:203
  144.8 24.2 %collective-permute-done.12.refs_0_ = bf16[4,128,1024]{2,1,0:T(8,128)(2,1)S(1)} collective-permute-done((bf16[4,128,1024]{2,1,0:T(8,128)(2,1)}, bf16[4,128,1024]{2,1,0:T(8,128)(2,1)S(1)}, u32[]{:S(2)}, u32[]{:S(2)}) %collective-permute-start.12) | collective-permute-done | bytes 1048608 | tf_op jit(solution)/shard_map/ppermute | solution.py:641
  169.0 3.2 collective-permute-start.18
  174.5 3.7 products.1
  178.3 9.9 %add_branch.2 = (f32[1024,1024]{1,0:T(8,128)}, bf16[1024,1024]{1,0:T(8,128)(2,1)S(1)}, bf16[1024,1024]{1,0:T(8,128)(2,1)S(1)}) custom-call(bf16[1024,1024]{1,0:T(8,128)(2,1)} %bitcast.319, bf16[1024,1024]{1,0:T(8,128)(2,1)} %constant_dynamic-slice_fusion.9.refs_0_.refs_1_.refs_3_, bf16[8,4,160,1024]{3,2,1,0:T(8,128)(2,1)} %bitcast.360, ...), custom_call_target="tpu_custom_call" | custom-call | tf_op jit(solution)/shard_map/add_branch/pallas_call | solution.py:399
  189.5 7.3 cross_forward.1
  200.0 3.8 pad_maximum_fusion
  203.8 7.5 add_branch.3
  211.3 11.6 %hidden_units.2 = (bf16[1024,2048]{1,0:T(8,128)(2,1)}, bf16[1024,2048]{1,0:T(8,128)(2,1)}) custom-call(bf16[1024,1024]{1,0:T(8,128)(2,1)S(1)} %get-tuple-element.95.normed_ref, bf16[2048,1024]{1,0:T(8,128)(2,1)} %bitcast.46.weight_ref.refs_4_, f32[1,2048]{1,0:T(1,128)S(1)} %bitcast.350), custom_call_target="tpu_custom_call" | custom-call | tf_op jit(solution)/shard_map/hidden_units/pallas_call | solution.py:532
  222.9 3.8 pad_maximum_fusion.1.refs_3_.weight_ref
  227.8 10.9 %hidden_units.3 = (bf16[1024,2048]{1,0:T(8,128)(2,1)}, bf16[1024,2048]{1,0:T(8,128)(2,1)}) custom-call(bf16[1024,1024]{1,0:T(8,128)(2,1)S(1)} %get-tuple-element.95.normed_ref, bf16[2048,1024]{1,0:T(8,128)(2,1)} %bitcast.52.weight_ref.refs_5_, f32[1,2048]{1,0:T(1,128)S(1)} %bitcast.351), custom_call_target="tpu_custom_call" | custom-call | tf_op jit(solution)/shard_map/hidden_units/pallas_call | solution.py:532
  238.6 14.1 %layer_output.1.refs_1_ = bf16[1024,1024]{1,0:T(8,128)(2,1)S(1)} custom-call(bf16[1024,2048]{1,0:T(8,128)(2,1)} %get-tuple-element.103.refs_3_.refs_0_.active_ref, bf16[1024,2048]{1,0:T(8,128)(2,1)} %get-tuple-element.104.refs_1_.active_ref, f32[1024,1024]{1,0:T(8,128)} %get-tuple-element.105.refs_2_, ...), custom_call_target="tpu_custom_call" | custom-call | tf_op jit(solution)/shard_map/layer_output/pallas_call | solution.py:399
  258.9 17.3 %units_grad.3 = (bf16[1024,2048]{1,0:T(8,128)(2,1)}, bf16[2048,1024]{1,0:T(8,128)(2,1)}, bf16[2048,1024]{1,0:T(8,128)(2,1)}, f32[1,2048]{1,0:T(1,128)S(1)}) custom-call(bf16[1024,2048]{1,0:T(8,128)(2,1)} %get-tuple-element.104.refs_1_.active_ref, bf16[1024,2048]{1,0:T(8,128)(2,1)} %tie.18.slope_ref, ...), custom_call_target="tpu_custom_call" | custom-call | tf_op jit(solution)/shard_map/units_grad/pallas_call | solution.py:560
  276.8 17.1 %units_grad.2 = (bf16[1024,2048]{1,0:T(8,128)(2,1)}, bf16[2048,1024]{1,0:T(8,128)(2,1)}, bf16[2048,1024]{1,0:T(8,128)(2,1)}, f32[1,2048]{1,0:T(1,128)S(1)}) custom-call(bf16[1024,2048]{1,0:T(8,128)(2,1)} %get-tuple-element.103.refs_3_.refs_0_.active_ref, bf16[1024,2048]{1,0:T(8,128)(2,1)} %get-tuple-element.109.slope_ref, ...), custom_call_target="tpu_custom_call" | custom-call | tf_op jit(solution)/shard_map/units_grad/pallas_call | solution.py:560
  295.8 4.6 fusion.1
  301.0 4.1 fusion
  308.8 21.0 %norm_grad.3 = (bf16[1024,1024]{1,0:T(8,128)(2,1)S(1)}, f32[1024,1024]{1,0:T(8,128)}, bf16[1024,1024]{1,0:T(8,128)(2,1)S(1)}, f32[8,1024]{1,0:T(8,128)S(1)}) custom-call(bf16[1024,2048]{1,0:T(8,128)(2,1)} %get-tuple-element.110.refs_0_, bf16[1024,2048]{1,0:T(8,128)(2,1)} %get-tuple-element.112.refs_1_, f32[1024,1024]{1,0:T(8,128)} %get-tuple-element.105.refs_2_, ...), custom_call_target="tpu_custom_call" | custom-call | tf_op jit(solution)/shard_map/norm_grad/pallas_call | solution.py:399
  331.7 16.5 %collective-permute-done.22.refs_0_ = bf16[2,4,128,1024]{3,2,1,0:T(8,128)(2,1)} collective-permute-done((bf16[2,4,128,1024]{3,2,1,0:T(8,128)(2,1)}, bf16[2,4,128,1024]{3,2,1,0:T(8,128)(2,1)}, u32[]{:S(2)}, u32[]{:S(2)}) %collective-permute-start.22) | collective-permute-done | bytes 2097184 | tf_op jit(solution)/shard_map/ppermute | solution.py:641
  348.3 3.5 fusion.5
  353.3 3.3 fusion.2
  359.9 11.1 %cross_backward.1 = (bf16[1,1024,1024]{2,1,0:T(8,128)(2,1)S(1)}, bf16[1,128,1024]{2,1,0:T(8,128)(2,1)S(1)}, bf16[1,128,1024]{2,1,0:T(8,128)(2,1)S(1)}) custom-call(s32[1]{0:T(128)} %dynamic_slice.54.lengths_ref, bf16[1,1024,1024]{2,1,0:T(8,128)(2,1)S(1)} %bitcast.328, bf16[1,128,1024]{2,1,0:T(8,128)(2,1)S(1)} %bitcast.341, ...), custom_call_target="tpu_custom_call" | custom-call | tf_op jit(solution)/shard_map/cross_backward/pallas_call | solution.py:272
  372.3 11.3 %deal_grads.2 = (bf16[4,4,2,32,1024]{4,3,2,1,0:T(8,128)(2,1)S(1)}, bf16[4,4,2,32,1024]{4,3,2,1,0:T(8,128)(2,1)}, bf16[4,4,2,32,1024]{4,3,2,1,0:T(8,128)(2,1)}, bf16[4,4,2,32,1024]{4,3,2,1,0:T(8,128)(2,1)}) custom-call(s32[1]{0:T(128)} %bitcast.76.own_ref, bf16[1024,1024]{1,0:T(8,128)(2,1)} %bitcast.321, bf16[1024,1024]{1,0:T(8,128)(2,1)} %copy-done.29, ...), custom_call_target="tpu_custom_call" | custom-call | tf_op jit(solution)/shard_map/deal_grads/pallas_call | solution.py:609
  385.4 3.7 sum_products.1.refs_2_
  389.1 11.6 %collective-permute-start.26 = (bf16[1,128,1024]{2,1,0:T(8,128)(2,1)}, bf16[1,128,1024]{2,1,0:T(8,128)(2,1)S(1)}, u32[]{:S(2)}, u32[]{:S(2)}) collective-permute-start(bf16[1,128,1024]{2,1,0:T(8,128)(2,1)} %bitcast.87), channel_id=1, source_target_pairs={{0,2},{1,3},{2,0},{3,1},{4,6},{5,7},{6,4},{7,5},{8,10},{9,11},{10,... | collective-permute-start | bytes 786440 | tf_op jit(solution)/shard_map/ppermute | solution.py:641
  400.7 3.2 fusion.7
  403.9 2.8 fusion.4
  409.2 11.8 %norm_grad.4 = (bf16[1024,1024]{1,0:T(8,128)(2,1)S(1)}, f32[1024,1024]{1,0:T(8,128)}, bf16[1024,1024]{1,0:T(8,128)(2,1)S(1)}, f32[8,1024]{1,0:T(8,128)S(1)}) custom-call(bf16[1024,1024]{1,0:T(8,128)(2,1)} %bitcast.326, f32[1024,1024]{1,0:T(8,128)} %get-tuple-element.94.refs_1_, f32[1024,1024]{1,0:T(8,128)} %get-tuple-element.122.refs_2_, ...), custom_call_target="tpu_custom_call" | custom-call | tf_op jit(solution)/shard_map/norm_grad/pallas_call | solution.py:399
  424.4 2.9 fusion.8
  428.9 2.6 add_convert_fusion.3
  436.9 47.0 %self_backward.1 = (bf16[1,1024,1024]{2,1,0:T(8,128)(2,1)S(1)}, bf16[1,1024,1024]{2,1,0:T(8,128)(2,1)S(1)}, bf16[1,1024,1024]{2,1,0:T(8,128)(2,1)}) custom-call(bf16[1,1024,1024]{2,1,0:T(8,128)(2,1)} %bitcast.330, bf16[1,1024,1024]{2,1,0:T(8,128)(2,1)} %bitcast.397, bf16[1,1024,1024]{2,1,0:T(8,128)(2,1)} %bitcast.399, bf16[1,1024,1024]{2,1,0:T(8,128)(2,1)} %bitcast.335, ...), custom_call_target="tpu_custom_call" | custom-call | tf_op jit(solution)/shard_map/self_backward/pallas_call | solution.py:223
  491.5 14.8 %norm_grad.5 = (bf16[1024,1024]{1,0:T(8,128)(2,1)S(1)}, f32[8,1024]{1,0:T(8,128)S(1)}) custom-call(bf16[1024,1024]{1,0:T(8,128)(2,1)S(1)} %bitcast.315, bf16[1024,1024]{1,0:T(8,128)(2,1)} %bitcast.323, bf16[1024,1024]{1,0:T(8,128)(2,1)} %bitcast.377, bf16[1024,1024]{1,0:T(8,128)(2,1)} %constant_dynamic-slice_fusion.9.refs_0_.refs_1_.refs_3_, ...), custom_call_target="tpu_custom_call" | custom-call | tf_op jit(solution)/shard_map/norm_grad/pallas_call | solution.py:399
  513.3 2.6 fusion.21
  516.5 49.1 %collective-permute-done.40.refs_0_ = bf16[256,1024]{1,0:T(8,128)(2,1)} collective-permute-done((bf16[256,1024]{1,0:T(8,128)(2,1)S(1)}, bf16[256,1024]{1,0:T(8,128)(2,1)}, u32[]{:S(2)}, u32[]{:S(2)}) %collective-permute-start.40) | collective-permute-done | bytes 524320 | tf_op jit(solution)/shard_map/ppermute | solution.py:641
  565.6 2.4 fusion.15.refs_3_
  574.2 16.8 %deal_grads.3 = (bf16[4,4,2,32,1024]{4,3,2,1,0:T(8,128)(2,1)S(1)}, bf16[4,4,2,32,1024]{4,3,2,1,0:T(8,128)(2,1)}, bf16[4,4,2,32,1024]{4,3,2,1,0:T(8,128)(2,1)}, bf16[4,4,2,32,1024]{4,3,2,1,0:T(8,128)(2,1)}) custom-call(s32[1]{0:T(128)} %bitcast.76.own_ref, bf16[1024,1024]{1,0:T(8,128)(2,1)} %bitcast.314, bf16[1024,1024]{1,0:T(8,128)(2,1)} %copy-done.4, ...), custom_call_target="tpu_custom_call" | custom-call | tf_op jit(solution)/shard_map/deal_grads/pallas_call | solution.py:609
  591.7 3.9 collective-permute-done.44
  595.6 2.9 add_convert_fusion.1
  601.8 2.6 fusion.9
  607.1 4.9 collective-permute-done.34
  626.7 5.4 collective-permute-done.36
  634.2 6.8 collective-permute-done.37
  644.2 2.5 fusion.22
  648.5 8.4 %collective-permute-done.61.refs_2_ = bf16[256,1024]{1,0:T(8,128)(2,1)} collective-permute-done((bf16[256,1024]{1,0:T(8,128)(2,1)S(1)}, bf16[256,1024]{1,0:T(8,128)(2,1)}, u32[]{:S(2)}, u32[]{:S(2)}) %collective-permute-start.61) | collective-permute-done | bytes 524320 | tf_op jit(solution)/shard_map/ppermute | solution.py:641
  656.9 29.8 %collective-permute-done.53.refs_0_ = bf16[2,128,1024]{2,1,0:T(8,128)(2,1)} collective-permute-done((bf16[2,128,1024]{2,1,0:T(8,128)(2,1)}, bf16[2,128,1024]{2,1,0:T(8,128)(2,1)}, u32[]{:S(2)}, u32[]{:S(2)}) %collective-permute-start.53) | collective-permute-done | bytes 524320 | tf_op jit(solution)/shard_map/ppermute | solution.py:641
  692.2 8.1 %collective-permute-done.43 = bf16[4,2,32,1024]{3,2,1,0:T(8,128)(2,1)S(1)} collective-permute-done((bf16[4,2,32,1024]{3,2,1,0:T(8,128)(2,1)S(1)}, bf16[4,2,32,1024]{3,2,1,0:T(8,128)(2,1)S(1)}, u32[]{:S(2)}, u32[]{:S(2)}) %collective-permute-start.43) | collective-permute-done | bytes 524320 | tf_op jit(solution)/shard_map/ppermute | solution.py:641
  702.7 2.6 pad_maximum_fusion.3
  710.8 3.9 collective-permute-done.47
  716.7 6.2 collective-permute-done.56
  723.1 4.1 collective-permute-done.48
  734.5 2.9 collective-permute-done.49
  737.5 6.3 collective-permute-done.50
  753.7 3.4 finish.18
  757.1 3.1 finish.19
  (457 shorter events, 181.2 us)
Async XLA Ops:
  7.2 78.6 %all-gather.17.cloned.1.call-start = ((), (), s32[]{:S(2)}) async-start(), calls=%async_computation.4 | async-start | bytes 7077888 | tf_op jit(solution)/shard_map/all_gather | solution.py:884
  12.4 11.4 %collective-permute-start = (bf16[96,1024]{1,0:T(8,128)(2,1)S(1)}, bf16[96,1024]{1,0:T(8,128)(2,1)S(1)}, u32[]{:S(2)}, u32[]{:S(2)}) collective-permute-start(bf16[96,1024]{1,0:T(8,128)(2,1)S(1)} %get-tuple-element.160), channel_id=1, source_target_pairs={{0,1},{1,0},{2,3},{3,2},{4,5},{5,4},{6,7},{7,6},{8,9},{9,8},{10,11... | collective-permute-start | bytes 589832 | tf_op jit(solution)/shard_map/ppermute | solution.py:641
  15.5 17.2 %collective-permute-start.1 = (bf16[96,1024]{1,0:T(8,128)(2,1)S(1)}, bf16[96,1024]{1,0:T(8,128)(2,1)S(1)}, u32[]{:S(2)}, u32[]{:S(2)}) collective-permute-start(bf16[96,1024]{1,0:T(8,128)(2,1)S(1)} %get-tuple-element.160), channel_id=1, source_target_pairs={{0,2},{1,3},{2,0},{3,1},{4,6},{5,7},{6,4},{7,5},{8,10},{9,11},{10,... | collective-permute-start | bytes 589832 | tf_op jit(solution)/shard_map/ppermute | solution.py:641
  18.1 14.6 %collective-permute-start.2 = (bf16[96,1024]{1,0:T(8,128)(2,1)S(1)}, bf16[96,1024]{1,0:T(8,128)(2,1)S(1)}, u32[]{:S(2)}, u32[]{:S(2)}) collective-permute-start(bf16[96,1024]{1,0:T(8,128)(2,1)S(1)} %get-tuple-element.160), channel_id=1, source_target_pairs={{0,3},{1,2},{2,1},{3,0},{4,7},{5,6},{6,5},{7,4},{8,11},{9,10},{10,... | collective-permute-start | bytes 589832 | tf_op jit(solution)/shard_map/ppermute | solution.py:641
  33.7 140.7 %all-gather.19.cloned.1.call-start = ((), (), s32[]{:S(2)}) async-start(), calls=%async_computation.5 | async-start | bytes 11796480 | tf_op jit(solution)/shard_map/all_gather | solution.py:901
  38.5 15.6 %collective-permute-start.6 = (bf16[160,1024]{1,0:T(8,128)(2,1)S(1)}, bf16[160,1024]{1,0:T(8,128)(2,1)S(1)}, u32[]{:S(2)}, u32[]{:S(2)}) collective-permute-start(bf16[160,1024]{1,0:T(8,128)(2,1)S(1)} %dynamic-slice_dynamic-update-slice_fusion), channel_id=1, source_target_pairs={{0,1},{1,0},{2,3},{3,2},{4,5},{5,4},{6,7},{7,6},{8,9},{9,8},{10,11... | collective-permute-start | bytes 983048 | tf_op jit(solution)/shard_map/ppermute | solution.py:641
  41.9 25.6 %collective-permute-start.7 = (bf16[160,1024]{1,0:T(8,128)(2,1)S(1)}, bf16[160,1024]{1,0:T(8,128)(2,1)S(1)}, u32[]{:S(2)}, u32[]{:S(2)}) collective-permute-start(bf16[160,1024]{1,0:T(8,128)(2,1)S(1)} %dynamic-slice_dynamic-update-slice_fusion), channel_id=1, source_target_pairs={{0,2},{1,3},{2,0},{3,1},{4,6},{5,7},{6,4},{7,5},{8,10},{9,11},{10,... | collective-permute-start | bytes 983048 | tf_op jit(solution)/shard_map/ppermute | solution.py:641
  42.9 24.6 %collective-permute-start.8 = (bf16[160,1024]{1,0:T(8,128)(2,1)S(1)}, bf16[160,1024]{1,0:T(8,128)(2,1)S(1)}, u32[]{:S(2)}, u32[]{:S(2)}) collective-permute-start(bf16[160,1024]{1,0:T(8,128)(2,1)S(1)} %dynamic-slice_dynamic-update-slice_fusion), channel_id=1, source_target_pairs={{0,3},{1,2},{2,1},{3,0},{4,7},{5,6},{6,5},{7,4},{8,11},{9,10},{10,... | collective-permute-start | bytes 983048 | tf_op jit(solution)/shard_map/ppermute | solution.py:641
  68.7 339.3 %all-gather.11.cloned.1.call-start = ((), (), s32[]{:S(2)}) async-start(), calls=%async_computation.1 | async-start | bytes 5242880 | tf_op jit(solution)/shard_map/all_gather | solution.py:860
  68.8 12.8 %collective-permute-start.4 = (f32[1024]{0:T(1024)S(1)}, f32[1024]{0:T(1024)S(1)}, u32[]{:S(2)}, u32[]{:S(2)}) collective-permute-start(f32[1024]{0:T(1024)S(1)} %copy-done.92), channel_id=1, source_target_pairs={{0,2},{1,3},{2,0},{3,1},{4,6},{5,7},{6,4},{7,5},{8,10},{9,11},{10,... | collective-permute-start | bytes 12296 | tf_op jit(solution)/shard_map/ppermute | solution.py:641
  74.9 10.4 %collective-permute-start.5 = (f32[1024]{0:T(1024)S(1)}, f32[1024]{0:T(1024)S(1)}, u32[]{:S(2)}, u32[]{:S(2)}) collective-permute-start(f32[1024]{0:T(1024)S(1)} %copy-done.92), channel_id=1, source_target_pairs={{0,3},{1,2},{2,1},{3,0},{4,7},{5,6},{6,5},{7,4},{8,11},{9,10},{10,... | collective-permute-start | bytes 12296 | tf_op jit(solution)/shard_map/ppermute | solution.py:641
  76.2 9.0 %collective-permute-start.3 = (f32[1024]{0:T(1024)S(1)}, f32[1024]{0:T(1024)S(1)}, u32[]{:S(2)}, u32[]{:S(2)}) collective-permute-start(f32[1024]{0:T(1024)S(1)} %copy-done.92), channel_id=1, source_target_pairs={{0,1},{1,0},{2,3},{3,2},{4,5},{5,4},{6,7},{7,6},{8,9},{9,8},{10,11... | collective-permute-start | bytes 12296 | tf_op jit(solution)/shard_map/ppermute | solution.py:641
  77.1 55.5 %collective-permute-start.10 = (bf16[128,1024]{1,0:T(8,128)(2,1)}, bf16[128,1024]{1,0:T(8,128)(2,1)S(1)}, u32[]{:S(2)}, u32[]{:S(2)}) collective-permute-start(bf16[128,1024]{1,0:T(8,128)(2,1)} %tie.15), channel_id=1, source_target_pairs={{0,2},{1,3},{2,0},{3,1},{4,6},{5,7},{6,4},{7,5},{8,10},{9,11},{10,... | collective-permute-start | bytes 786440 | tf_op jit(solution)/shard_map/ppermute | solution.py:641
  80.2 52.4 %collective-permute-start.11 = (bf16[128,1024]{1,0:T(8,128)(2,1)}, bf16[128,1024]{1,0:T(8,128)(2,1)S(1)}, u32[]{:S(2)}, u32[]{:S(2)}) collective-permute-start(bf16[128,1024]{1,0:T(8,128)(2,1)} %tie.15), channel_id=1, source_target_pairs={{0,3},{1,2},{2,1},{3,0},{4,7},{5,6},{6,5},{7,4},{8,11},{9,10},{10,... | collective-permute-start | bytes 786440 | tf_op jit(solution)/shard_map/ppermute | solution.py:641
  81.5 51.1 %collective-permute-start.9 = (bf16[128,1024]{1,0:T(8,128)(2,1)}, bf16[128,1024]{1,0:T(8,128)(2,1)S(1)}, u32[]{:S(2)}, u32[]{:S(2)}) collective-permute-start(bf16[128,1024]{1,0:T(8,128)(2,1)} %tie.15), channel_id=1, source_target_pairs={{0,1},{1,0},{2,3},{3,2},{4,5},{5,4},{6,7},{7,6},{8,9},{9,8},{10,11... | collective-permute-start | bytes 786440 | tf_op jit(solution)/shard_map/ppermute | solution.py:641
  135.9 33.1 %collective-permute-start.12 = (bf16[4,128,1024]{2,1,0:T(8,128)(2,1)}, bf16[4,128,1024]{2,1,0:T(8,128)(2,1)S(1)}, u32[]{:S(2)}, u32[]{:S(2)}) collective-permute-start(bf16[4,128,1024]{2,1,0:T(8,128)(2,1)} %tie.16), channel_id=1, source_target_pairs={{0,8},{4,12},{8,0},{12,4},{16,24},{20,28},{24,16},{28,20},{1,9},{5... | collective-permute-start | bytes 3145736 | tf_op jit(solution)/shard_map/ppermute | solution.py:641
  137.4 61.4 %collective-permute-start.13 = (bf16[4,128,1024]{2,1,0:T(8,128)(2,1)}, bf16[4,128,1024]{2,1,0:T(8,128)(2,1)}, u32[]{:S(2)}, u32[]{:S(2)}) collective-permute-start(bf16[4,128,1024]{2,1,0:T(8,128)(2,1)} %tie.16), channel_id=1, source_target_pairs={{0,16},{4,20},{8,24},{12,28},{16,0},{20,4},{24,8},{28,12},{1,17},{... | collective-permute-start | bytes 3145736 | tf_op jit(solution)/shard_map/ppermute | solution.py:641
  138.9 59.8 %collective-permute-start.14 = (bf16[4,128,1024]{2,1,0:T(8,128)(2,1)}, bf16[4,128,1024]{2,1,0:T(8,128)(2,1)}, u32[]{:S(2)}, u32[]{:S(2)}) collective-permute-start(bf16[4,128,1024]{2,1,0:T(8,128)(2,1)} %tie.16), channel_id=1, source_target_pairs={{0,24},{4,28},{8,16},{12,20},{16,8},{20,12},{24,0},{28,4},{1,25},{... | collective-permute-start | bytes 3145736 | tf_op jit(solution)/shard_map/ppermute | solution.py:641
  141.8 81.1 %collective-permute-start.16 = (bf16[4,128,1024]{2,1,0:T(8,128)(2,1)}, bf16[4,128,1024]{2,1,0:T(8,128)(2,1)}, u32[]{:S(2)}, u32[]{:S(2)}) collective-permute-start(bf16[4,128,1024]{2,1,0:T(8,128)(2,1)} %tie.17), channel_id=1, source_target_pairs={{0,1},{1,0},{2,3},{3,2},{4,5},{5,4},{6,7},{7,6},{8,9},{9,8},{10,11... | collective-permute-start | bytes 3145736 | tf_op jit(solution)/shard_map/ppermute | solution.py:641
  143.8 79.1 %collective-permute-start.17 = (bf16[4,128,1024]{2,1,0:T(8,128)(2,1)}, bf16[4,128,1024]{2,1,0:T(8,128)(2,1)}, u32[]{:S(2)}, u32[]{:S(2)}) collective-permute-start(bf16[4,128,1024]{2,1,0:T(8,128)(2,1)} %tie.17), channel_id=1, source_target_pairs={{0,2},{1,3},{2,0},{3,1},{4,6},{5,7},{6,4},{7,5},{8,10},{9,11},{10,... | collective-permute-start | bytes 3145736 | tf_op jit(solution)/shard_map/ppermute | solution.py:641
  169.0 53.8 %collective-permute-start.18 = (bf16[4,128,1024]{2,1,0:T(8,128)(2,1)}, bf16[4,128,1024]{2,1,0:T(8,128)(2,1)}, u32[]{:S(2)}, u32[]{:S(2)}) collective-permute-start(bf16[4,128,1024]{2,1,0:T(8,128)(2,1)} %tie.17), channel_id=1, source_target_pairs={{0,3},{1,2},{2,1},{3,0},{4,7},{5,6},{6,5},{7,4},{8,11},{9,10},{10,... | collective-permute-start | bytes 3145736 | tf_op jit(solution)/shard_map/ppermute | solution.py:641
  203.8 24.0 %collective-permute-start.15 = (bf16[4,4,128,1024]{3,2,1,0:T(8,128)(2,1)}, bf16[4,4,128,1024]{3,2,1,0:T(8,128)(2,1)}, u32[]{:S(2)}, u32[]{:S(2)}) collective-permute-start(bf16[4,4,128,1024]{3,2,1,0:T(8,128)(2,1)} %pad_maximum_fusion), channel_id=1, source_target_pairs={{0,4},{4,0},{8,12},{12,8},{16,20},{20,16},{24,28},{28,24},{1,5},{5... | collective-permute-start | bytes 12582920 | tf_op jit(solution)/shard_map/ppermute | solution.py:641
  226.7 12.0 %collective-permute-start.19 = (bf16[4,4,128,1024]{3,2,1,0:T(8,128)(2,1)}, bf16[4,4,128,1024]{3,2,1,0:T(8,128)(2,1)}, u32[]{:S(2)}, u32[]{:S(2)}) collective-permute-start(bf16[4,4,128,1024]{3,2,1,0:T(8,128)(2,1)} %pad_maximum_fusion.1.refs_3_.weight_ref), channel_id=1, source_target_pairs={{0,4},{4,0},{8,12},{12,8},{16,20},{20,16},{24,28},{28,24},{1,5},{5... | collective-permute-start | bytes 12582920 | tf_op jit(solution)/shard_map/ppermute | solution.py:641
  254.7 234.5 %all-gather.9.cloned.1.call-start = ((), (), s32[]{:S(2)}) async-start(), calls=%async_computation | async-start | bytes 5242880 | tf_op jit(solution)/shard_map/all_gather | solution.py:860
  276.2 19.5 %collective-permute-start.20 = (bf16[4,4,128,1024]{3,2,1,0:T(8,128)(2,1)}, bf16[4,4,128,1024]{3,2,1,0:T(8,128)(2,1)}, u32[]{:S(2)}, u32[]{:S(2)}) collective-permute-start(bf16[4,4,128,1024]{3,2,1,0:T(8,128)(2,1)} %bitcast.467), channel_id=1, source_target_pairs={{0,4},{4,0},{8,12},{12,8},{16,20},{20,16},{24,28},{28,24},{1,5},{5... | collective-permute-start | bytes 12582920 | tf_op jit(solution)/shard_map/ppermute | solution.py:641
  276.3 24.7 %collective-permute-start.21 = (bf16[4,4,128,1024]{3,2,1,0:T(8,128)(2,1)}, bf16[4,4,128,1024]{3,2,1,0:T(8,128)(2,1)}, u32[]{:S(2)}, u32[]{:S(2)}) collective-permute-start(bf16[4,4,128,1024]{3,2,1,0:T(8,128)(2,1)} %bitcast.466), channel_id=1, source_target_pairs={{0,4},{4,0},{8,12},{12,8},{16,20},{20,16},{24,28},{28,24},{1,5},{5... | collective-permute-start | bytes 12582920 | tf_op jit(solution)/shard_map/ppermute | solution.py:641
  295.7 464.6 %all-gather.15.cloned.1.call-start = ((), (), s32[]{:S(2)}) async-start(), calls=%async_computation.3 | async-start | bytes 5242880 | tf_op jit(solution)/shard_map/all_gather | solution.py:860
  300.4 47.9 %collective-permute-start.22 = (bf16[2,4,128,1024]{3,2,1,0:T(8,128)(2,1)}, bf16[2,4,128,1024]{3,2,1,0:T(8,128)(2,1)}, u32[]{:S(2)}, u32[]{:S(2)}) collective-permute-start(bf16[2,4,128,1024]{3,2,1,0:T(8,128)(2,1)} %fusion.1), channel_id=1, source_target_pairs={{0,8},{4,12},{8,0},{12,4},{16,24},{20,28},{24,16},{28,20},{1,9},{5... | collective-permute-start | bytes 6291464 | tf_op jit(solution)/shard_map/ppermute | solution.py:641
  305.1 48.2 %collective-permute-start.23 = (bf16[2,4,128,1024]{3,2,1,0:T(8,128)(2,1)}, bf16[2,4,128,1024]{3,2,1,0:T(8,128)(2,1)}, u32[]{:S(2)}, u32[]{:S(2)}) collective-permute-start(bf16[2,4,128,1024]{3,2,1,0:T(8,128)(2,1)} %fusion), channel_id=1, source_target_pairs={{0,16},{4,20},{8,24},{12,28},{16,0},{20,4},{24,8},{28,12},{1,17},{... | collective-permute-start | bytes 6291464 | tf_op jit(solution)/shard_map/ppermute | solution.py:641
  351.7 49.0 %collective-permute-start.24 = (bf16[4,128,1024]{2,1,0:T(8,128)(2,1)}, bf16[4,128,1024]{2,1,0:T(8,128)(2,1)}, u32[]{:S(2)}, u32[]{:S(2)}) collective-permute-start(bf16[4,128,1024]{2,1,0:T(8,128)(2,1)} %fusion.5), channel_id=1, source_target_pairs={{0,16},{4,20},{8,24},{12,28},{16,0},{20,4},{24,8},{28,12},{1,17},{... | collective-permute-start | bytes 3145736 | tf_op jit(solution)/shard_map/ppermute | solution.py:641
  356.6 44.1 %collective-permute-start.25 = (bf16[4,128,1024]{2,1,0:T(8,128)(2,1)}, bf16[4,128,1024]{2,1,0:T(8,128)(2,1)}, u32[]{:S(2)}, u32[]{:S(2)}) collective-permute-start(bf16[4,128,1024]{2,1,0:T(8,128)(2,1)} %fusion.2), channel_id=1, source_target_pairs={{0,8},{4,12},{8,0},{12,4},{16,24},{20,28},{24,16},{28,20},{1,9},{5... | collective-permute-start | bytes 3145736 | tf_op jit(solution)/shard_map/ppermute | solution.py:641
  384.9 38.0 %collective-permute-start.27 = (bf16[4,4,2,32,1024]{4,3,2,1,0:T(8,128)(2,1)}, bf16[4,4,2,32,1024]{4,3,2,1,0:T(8,128)(2,1)}, u32[]{:S(2)}, u32[]{:S(2)}) collective-permute-start(bf16[4,4,2,32,1024]{4,3,2,1,0:T(8,128)(2,1)} %get-tuple-element.127.refs_1_), channel_id=1, source_target_pairs={{0,4},{4,0},{8,12},{12,8},{16,20},{20,16},{24,28},{28,24},{1,5},{5... | collective-permute-start | bytes 6291464 | tf_op jit(solution)/shard_map/ppermute | solution.py:641
  384.9 43.1 %collective-permute-start.28 = (bf16[4,4,2,32,1024]{4,3,2,1,0:T(8,128)(2,1)}, bf16[4,4,2,32,1024]{4,3,2,1,0:T(8,128)(2,1)}, u32[]{:S(2)}, u32[]{:S(2)}) collective-permute-start(bf16[4,4,2,32,1024]{4,3,2,1,0:T(8,128)(2,1)} %get-tuple-element.131), channel_id=1, source_target_pairs={{0,4},{4,0},{8,12},{12,8},{16,20},{20,16},{24,28},{28,24},{1,5},{5... | collective-permute-start | bytes 6291464 | tf_op jit(solution)/shard_map/ppermute | solution.py:641
  389.1 43.6 %collective-permute-start.26 = (bf16[1,128,1024]{2,1,0:T(8,128)(2,1)}, bf16[1,128,1024]{2,1,0:T(8,128)(2,1)S(1)}, u32[]{:S(2)}, u32[]{:S(2)}) collective-permute-start(bf16[1,128,1024]{2,1,0:T(8,128)(2,1)} %bitcast.87), channel_id=1, source_target_pairs={{0,2},{1,3},{2,0},{3,1},{4,6},{5,7},{6,4},{7,5},{8,10},{9,11},{10,... | collective-permute-start | bytes 786440 | tf_op jit(solution)/shard_map/ppermute | solution.py:641
  408.0 78.0 %collective-permute-start.31 = (bf16[2,256,1024]{2,1,0:T(8,128)(2,1)}, bf16[2,256,1024]{2,1,0:T(8,128)(2,1)}, u32[]{:S(2)}, u32[]{:S(2)}) collective-permute-start(bf16[2,256,1024]{2,1,0:T(8,128)(2,1)} %slice_bitcast_fusion.2), channel_id=1, source_target_pairs={{0,1},{1,0},{2,3},{3,2},{4,5},{5,4},{6,7},{7,6},{8,9},{9,8},{10,11... | collective-permute-start | bytes 3145736 | tf_op jit(solution)/shard_map/ppermute | solution.py:641
  427.3 61.9 %collective-permute-start.29 = (bf16[2,4,2,32,1024]{4,3,2,1,0:T(8,128)(2,1)}, bf16[2,4,2,32,1024]{4,3,2,1,0:T(8,128)(2,1)}, u32[]{:S(2)}, u32[]{:S(2)}) collective-permute-start(bf16[2,4,2,32,1024]{4,3,2,1,0:T(8,128)(2,1)} %fusion.8), channel_id=1, source_target_pairs={{0,8},{4,12},{8,0},{12,4},{16,24},{20,28},{24,16},{28,20},{1,9},{5... | collective-permute-start | bytes 3145736 | tf_op jit(solution)/shard_map/ppermute | solution.py:641
  431.5 57.7 %collective-permute-start.30 = (bf16[2,4,2,32,1024]{4,3,2,1,0:T(8,128)(2,1)}, bf16[2,4,2,32,1024]{4,3,2,1,0:T(8,128)(2,1)}, u32[]{:S(2)}, u32[]{:S(2)}) collective-permute-start(bf16[2,4,2,32,1024]{4,3,2,1,0:T(8,128)(2,1)} %add_convert_fusion.3), channel_id=1, source_target_pairs={{0,16},{4,20},{8,24},{12,28},{16,0},{20,4},{24,8},{28,12},{1,17},{... | collective-permute-start | bytes 3145736 | tf_op jit(solution)/shard_map/ppermute | solution.py:641
  434.5 50.7 %collective-permute-start.32 = (bf16[2,128,1024]{2,1,0:T(8,128)(2,1)S(1)}, bf16[2,128,1024]{2,1,0:T(8,128)(2,1)S(1)}, u32[]{:S(2)}, u32[]{:S(2)}) collective-permute-start(bf16[2,128,1024]{2,1,0:T(8,128)(2,1)S(1)} %pad_maximum_fusion.12.refs_1_), channel_id=1, source_target_pairs={{0,1},{1,0},{2,3},{3,2},{4,5},{5,4},{6,7},{7,6},{8,9},{9,8},{10,11... | collective-permute-start | bytes 1572872 | tf_op jit(solution)/shard_map/ppermute | solution.py:641
  507.8 258.3 %all-gather.13.cloned.1.call-start = ((), (), s32[]{:S(2)}) async-start(), calls=%async_computation.2 | async-start | bytes 5242880 | tf_op jit(solution)/shard_map/all_gather | solution.py:860
  509.4 56.2 %collective-permute-start.40 = (bf16[256,1024]{1,0:T(8,128)(2,1)S(1)}, bf16[256,1024]{1,0:T(8,128)(2,1)}, u32[]{:S(2)}, u32[]{:S(2)}) collective-permute-start(bf16[256,1024]{1,0:T(8,128)(2,1)S(1)} %fusion.13), channel_id=1, source_target_pairs={{0,2},{1,3},{2,0},{3,1},{4,6},{5,7},{6,4},{7,5},{8,10},{9,11},{10,... | collective-permute-start | bytes 1572872 | tf_op jit(solution)/shard_map/ppermute | solution.py:641
  512.5 55.6 %collective-permute-start.38 = (bf16[4,2,32,1024]{3,2,1,0:T(8,128)(2,1)}, bf16[4,2,32,1024]{3,2,1,0:T(8,128)(2,1)S(1)}, u32[]{:S(2)}, u32[]{:S(2)}) collective-permute-start(bf16[4,2,32,1024]{3,2,1,0:T(8,128)(2,1)} %fusion.16), channel_id=1, source_target_pairs={{0,16},{4,20},{8,24},{12,28},{16,0},{20,4},{24,8},{28,12},{1,17},{... | collective-permute-start | bytes 1572872 | tf_op jit(solution)/shard_map/ppermute | solution.py:641
  515.9 53.0 %collective-permute-start.39 = (bf16[4,2,32,1024]{3,2,1,0:T(8,128)(2,1)}, bf16[4,2,32,1024]{3,2,1,0:T(8,128)(2,1)S(1)}, u32[]{:S(2)}, u32[]{:S(2)}) collective-permute-start(bf16[4,2,32,1024]{3,2,1,0:T(8,128)(2,1)} %fusion.21), channel_id=1, source_target_pairs={{0,8},{4,12},{8,0},{12,4},{16,24},{20,28},{24,16},{28,20},{1,9},{5... | collective-permute-start | bytes 1572872 | tf_op jit(solution)/shard_map/ppermute | solution.py:641
  591.1 10.7 %collective-permute-start.41 = (bf16[4,4,2,32,1024]{4,3,2,1,0:T(8,128)(2,1)}, bf16[4,4,2,32,1024]{4,3,2,1,0:T(8,128)(2,1)}, u32[]{:S(2)}, u32[]{:S(2)}) collective-permute-start(bf16[4,4,2,32,1024]{4,3,2,1,0:T(8,128)(2,1)} %get-tuple-element.143), channel_id=1, source_target_pairs={{0,4},{4,0},{8,12},{12,8},{16,20},{20,16},{24,28},{28,24},{1,5},{5... | collective-permute-start | bytes 6291464 | tf_op jit(solution)/shard_map/ppermute | solution.py:641
  598.5 43.6 %collective-permute-start.45 = (bf16[2,4,2,32,1024]{4,3,2,1,0:T(8,128)(2,1)}, bf16[2,4,2,32,1024]{4,3,2,1,0:T(8,128)(2,1)}, u32[]{:S(2)}, u32[]{:S(2)}) collective-permute-start(bf16[2,4,2,32,1024]{4,3,2,1,0:T(8,128)(2,1)} %add_convert_fusion.1), channel_id=1, source_target_pairs={{0,16},{4,20},{8,24},{12,28},{16,0},{20,4},{24,8},{28,12},{1,17},{... | collective-permute-start | bytes 3145736 | tf_op jit(solution)/shard_map/ppermute | solution.py:641
  604.4 82.2 %collective-permute-start.42 = (bf16[2,4,2,32,1024]{4,3,2,1,0:T(8,128)(2,1)}, bf16[2,4,2,32,1024]{4,3,2,1,0:T(8,128)(2,1)}, u32[]{:S(2)}, u32[]{:S(2)}) collective-permute-start(bf16[2,4,2,32,1024]{4,3,2,1,0:T(8,128)(2,1)} %fusion.9), channel_id=1, source_target_pairs={{0,8},{4,12},{8,0},{12,4},{16,24},{20,28},{24,16},{28,20},{1,9},{5... | collective-permute-start | bytes 3145736 | tf_op jit(solution)/shard_map/ppermute | solution.py:641
  613.3 18.8 %collective-permute-start.36 = (f32[13,1024]{1,0:T(8,128)S(1)}, f32[13,1024]{1,0:T(8,128)S(1)}, u32[]{:S(2)}, u32[]{:S(2)}) collective-permute-start(f32[13,1024]{1,0:T(8,128)S(1)} %add.319), channel_id=1, source_target_pairs={{0,8},{4,12},{8,0},{12,4},{16,24},{20,28},{24,16},{28,20},{1,9},{5... | collective-permute-start | bytes 159752 | tf_op jit(solution)/shard_map/ppermute | solution.py:641
  624.3 22.4 %collective-permute-start.59 = (bf16[256,1024]{1,0:T(8,128)(2,1)S(1)}, bf16[256,1024]{1,0:T(8,128)(2,1)S(1)}, u32[]{:S(2)}, u32[]{:S(2)}) collective-permute-start(bf16[256,1024]{1,0:T(8,128)(2,1)S(1)} %copy-done.66), channel_id=1, source_target_pairs={{0,8},{4,12},{8,0},{12,4},{16,24},{20,28},{24,16},{28,20},{1,9},{5... | collective-permute-start | bytes 1572872 | tf_op jit(solution)/shard_map/ppermute | solution.py:641
  626.2 22.3 %collective-permute-start.60 = (bf16[256,1024]{1,0:T(8,128)(2,1)S(1)}, bf16[256,1024]{1,0:T(8,128)(2,1)S(1)}, u32[]{:S(2)}, u32[]{:S(2)}) collective-permute-start(bf16[256,1024]{1,0:T(8,128)(2,1)S(1)} %copy-done.66), channel_id=1, source_target_pairs={{0,16},{4,20},{8,24},{12,28},{16,0},{20,4},{24,8},{28,12},{1,17},{... | collective-permute-start | bytes 1572872 | tf_op jit(solution)/shard_map/ppermute | solution.py:641
  641.0 15.9 %collective-permute-start.61 = (bf16[256,1024]{1,0:T(8,128)(2,1)S(1)}, bf16[256,1024]{1,0:T(8,128)(2,1)}, u32[]{:S(2)}, u32[]{:S(2)}) collective-permute-start(bf16[256,1024]{1,0:T(8,128)(2,1)S(1)} %copy-done.66), channel_id=1, source_target_pairs={{0,24},{4,28},{8,16},{12,20},{16,8},{20,12},{24,0},{28,4},{1,25},{... | collective-permute-start | bytes 1572872 | tf_op jit(solution)/shard_map/ppermute | solution.py:641
  642.1 44.5 %collective-permute-start.53 = (bf16[2,128,1024]{2,1,0:T(8,128)(2,1)}, bf16[2,128,1024]{2,1,0:T(8,128)(2,1)}, u32[]{:S(2)}, u32[]{:S(2)}) collective-permute-start(bf16[2,128,1024]{2,1,0:T(8,128)(2,1)} %fusion.24), channel_id=1, source_target_pairs={{0,1},{1,0},{2,3},{3,2},{4,5},{5,4},{6,7},{7,6},{8,9},{9,8},{10,11... | collective-permute-start | bytes 1572872 | tf_op jit(solution)/shard_map/ppermute | solution.py:641
  646.7 43.5 %collective-permute-start.46 = (bf16[4,2,32,1024]{3,2,1,0:T(8,128)(2,1)}, bf16[4,2,32,1024]{3,2,1,0:T(8,128)(2,1)}, u32[]{:S(2)}, u32[]{:S(2)}) collective-permute-start(bf16[4,2,32,1024]{3,2,1,0:T(8,128)(2,1)} %fusion.22), channel_id=1, source_target_pairs={{0,8},{4,12},{8,0},{12,4},{16,24},{20,28},{24,16},{28,20},{1,9},{5... | collective-permute-start | bytes 1572872 | tf_op jit(solution)/shard_map/ppermute | solution.py:641
  688.1 12.2 %collective-permute-start.43 = (bf16[4,2,32,1024]{3,2,1,0:T(8,128)(2,1)S(1)}, bf16[4,2,32,1024]{3,2,1,0:T(8,128)(2,1)S(1)}, u32[]{:S(2)}, u32[]{:S(2)}) collective-permute-start(bf16[4,2,32,1024]{3,2,1,0:T(8,128)(2,1)S(1)} %fusion.10), channel_id=1, source_target_pairs={{0,16},{4,20},{8,24},{12,28},{16,0},{20,4},{24,8},{28,12},{1,17},{... | collective-permute-start | bytes 1572872 | tf_op jit(solution)/shard_map/ppermute | solution.py:641
  690.1 15.8 %collective-permute-start.54 = (bf16[128,1024]{1,0:T(8,128)(2,1)S(1)}, bf16[128,1024]{1,0:T(8,128)(2,1)}, u32[]{:S(2)}, u32[]{:S(2)}) collective-permute-start(bf16[128,1024]{1,0:T(8,128)(2,1)S(1)} %fusion.27), channel_id=1, source_target_pairs={{0,2},{1,3},{2,0},{3,1},{4,6},{5,7},{6,4},{7,5},{8,10},{9,11},{10,... | collective-permute-start | bytes 786440 | tf_op jit(solution)/shard_map/ppermute | solution.py:641
  702.0 12.7 %collective-permute-start.47 = (bf16[2,128,1024]{2,1,0:T(8,128)(2,1)S(1)}, bf16[2,128,1024]{2,1,0:T(8,128)(2,1)}, u32[]{:S(2)}, u32[]{:S(2)}) collective-permute-start(bf16[2,128,1024]{2,1,0:T(8,128)(2,1)S(1)} %fusion.26), channel_id=1, source_target_pairs={{0,1},{1,0},{2,3},{3,2},{4,5},{5,4},{6,7},{7,6},{8,9},{9,8},{10,11... | collective-permute-start | bytes 1572872 | tf_op jit(solution)/shard_map/ppermute | solution.py:641
  705.3 46.6 %collective-permute-start.62 = (bf16[4,256,1024]{2,1,0:T(8,128)(2,1)}, bf16[4,256,1024]{2,1,0:T(8,128)(2,1)}, u32[]{:S(2)}, u32[]{:S(2)}) collective-permute-start(bf16[4,256,1024]{2,1,0:T(8,128)(2,1)} %pad_maximum_fusion.3), channel_id=1, source_target_pairs={{0,4},{4,0},{8,12},{12,8},{16,20},{20,16},{24,28},{28,24},{1,5},{5... | collective-permute-start | bytes 6291464 | tf_op jit(solution)/shard_map/ppermute | solution.py:641
  707.2 9.5 %collective-permute-start.55 = (bf16[128,1024]{1,0:T(8,128)(2,1)S(1)}, bf16[128,1024]{1,0:T(8,128)(2,1)S(1)}, u32[]{:S(2)}, u32[]{:S(2)}) collective-permute-start(bf16[128,1024]{1,0:T(8,128)(2,1)S(1)} %fusion.29), channel_id=1, source_target_pairs={{0,8},{4,12},{8,0},{12,4},{16,24},{20,28},{24,16},{28,20},{1,9},{5... | collective-permute-start | bytes 786440 | tf_op jit(solution)/shard_map/ppermute | solution.py:641
  708.8 14.0 %collective-permute-start.56 = (bf16[128,1024]{1,0:T(8,128)(2,1)S(1)}, bf16[128,1024]{1,0:T(8,128)(2,1)S(1)}, u32[]{:S(2)}, u32[]{:S(2)}) collective-permute-start(bf16[128,1024]{1,0:T(8,128)(2,1)S(1)} %fusion.29), channel_id=1, source_target_pairs={{0,16},{4,20},{8,24},{12,28},{16,0},{20,4},{24,8},{28,12},{1,17},{... | collective-permute-start | bytes 786440 | tf_op jit(solution)/shard_map/ppermute | solution.py:641
  710.4 12.5 %collective-permute-start.57 = (bf16[128,1024]{1,0:T(8,128)(2,1)S(1)}, bf16[128,1024]{1,0:T(8,128)(2,1)S(1)}, u32[]{:S(2)}, u32[]{:S(2)}) collective-permute-start(bf16[128,1024]{1,0:T(8,128)(2,1)S(1)} %fusion.29), channel_id=1, source_target_pairs={{0,24},{4,28},{8,16},{12,20},{16,8},{20,12},{24,0},{28,4},{1,25},{... | collective-permute-start | bytes 786440 | tf_op jit(solution)/shard_map/ppermute | solution.py:641
  715.7 11.5 %collective-permute-start.48 = (bf16[128,1024]{1,0:T(8,128)(2,1)S(1)}, bf16[128,1024]{1,0:T(8,128)(2,1)S(1)}, u32[]{:S(2)}, u32[]{:S(2)}) collective-permute-start(bf16[128,1024]{1,0:T(8,128)(2,1)S(1)} %fusion.30), channel_id=1, source_target_pairs={{0,2},{1,3},{2,0},{3,1},{4,6},{5,7},{6,4},{7,5},{8,10},{9,11},{10,... | collective-permute-start | bytes 786440 | tf_op jit(solution)/shard_map/ppermute | solution.py:641
  723.0 21.9 %collective-permute-start.58 = (bf16[4,128,1024]{2,1,0:T(8,128)(2,1)S(1)}, bf16[4,128,1024]{2,1,0:T(8,128)(2,1)S(1)}, u32[]{:S(2)}, u32[]{:S(2)}) collective-permute-start(bf16[4,128,1024]{2,1,0:T(8,128)(2,1)S(1)} %pad_maximum_fusion.10), channel_id=1, source_target_pairs={{0,4},{4,0},{8,12},{12,8},{16,20},{20,16},{24,28},{28,24},{1,5},{5... | collective-permute-start | bytes 3145736 | tf_op jit(solution)/shard_map/ppermute | solution.py:641
  728.2 9.2 %collective-permute-start.49 = (bf16[128,1024]{1,0:T(8,128)(2,1)S(1)}, bf16[128,1024]{1,0:T(8,128)(2,1)S(1)}, u32[]{:S(2)}, u32[]{:S(2)}) collective-permute-start(bf16[128,1024]{1,0:T(8,128)(2,1)S(1)} %fusion.32), channel_id=1, source_target_pairs={{0,8},{4,12},{8,0},{12,4},{16,24},{20,28},{24,16},{28,20},{1,9},{5... | collective-permute-start | bytes 786440 | tf_op jit(solution)/shard_map/ppermute | solution.py:641
  730.2 13.6 %collective-permute-start.50 = (bf16[128,1024]{1,0:T(8,128)(2,1)S(1)}, bf16[128,1024]{1,0:T(8,128)(2,1)S(1)}, u32[]{:S(2)}, u32[]{:S(2)}) collective-permute-start(bf16[128,1024]{1,0:T(8,128)(2,1)S(1)} %fusion.32), channel_id=1, source_target_pairs={{0,16},{4,20},{8,24},{12,28},{16,0},{20,4},{24,8},{28,12},{1,17},{... | collective-permute-start | bytes 786440 | tf_op jit(solution)/shard_map/ppermute | solution.py:641
  731.6 12.1 %collective-permute-start.51 = (bf16[128,1024]{1,0:T(8,128)(2,1)S(1)}, bf16[128,1024]{1,0:T(8,128)(2,1)S(1)}, u32[]{:S(2)}, u32[]{:S(2)}) collective-permute-start(bf16[128,1024]{1,0:T(8,128)(2,1)S(1)} %fusion.32), channel_id=1, source_target_pairs={{0,24},{4,28},{8,16},{12,20},{16,8},{20,12},{24,0},{28,4},{1,25},{... | collective-permute-start | bytes 786440 | tf_op jit(solution)/shard_map/ppermute | solution.py:641
  744.8 26.0 %collective-permute-start.52 = (bf16[4,128,1024]{2,1,0:T(8,128)(2,1)}, bf16[4,128,1024]{2,1,0:T(8,128)(2,1)S(1)}, u32[]{:S(2)}, u32[]{:S(2)}) collective-permute-start(bf16[4,128,1024]{2,1,0:T(8,128)(2,1)} %pad_maximum_fusion.9), channel_id=1, source_target_pairs={{0,4},{4,0},{8,12},{12,8},{16,20},{20,16},{24,28},{28,24},{1,5},{5... | collective-permute-start | bytes 3145736 | tf_op jit(solution)/shard_map/ppermute | solution.py:641
  (99 other events, 1159.1 us)
Sparse Core Ops, SparseCore 0:
  33.8 47.5 all-gather.16
  83.8 71.5 all-gather.18
  254.9 89.2 all-gather.10
  346.1 95.2 all-gather.8
  507.9 94.4 all-gather.14
  604.5 87.7 all-gather.12
